TPU v7x, 512 devices: a whole 4x8x8 slice. The times are simulated.
512 devices in a mesh: dp: 4 (over z_lo), ctx: 32 (over y, x), tp: 4 (over z_hi, core).
Axes of the slice: x: 4, y: 8, z: 8 (z_hi: 2, z_lo: 4; z = z_hi * 4 + z_lo), core: 2. Of those that a mesh axis runs over, the one named last changes fastest.
Arguments:
- residual_in: bfloat16 [24576, 1536], P(('dp', 'ctx')), parts along dimension 0, may hold values from -11 to 11
- queries: bfloat16 [24576, 1536], P(('dp', 'ctx'), 'tp'), parts along dimension 0, may hold values from -9 to 9
- keys: bfloat16 [24576, 1536], P(('dp', 'ctx'), 'tp'), parts along dimension 0, may hold values from -9 to 9
- values: bfloat16 [24576, 1536], P(('dp', 'ctx'), 'tp'), parts along dimension 0, may hold values from -6 to 6
- out_weight: bfloat16 [1536, 1536], P('tp'), may hold values from -0.15625 to 0.15625
- norm_gain: float32 [1536], replicated, may hold values from 0.1 to 1.9
- norm_bias: float32 [1536], replicated, may hold values from -2.5 to 2.5
- glu_weight: bfloat16 [1536, 2, 1536], P(None, None, 'tp'), may hold values from -0.15625 to 0.15625
- conv_weight: float32 [31, 1536], P(None, 'tp'), may hold values from -1 to 1
- conv_scale: float32 [1536], P('tp'), may hold values from 0.1 to 1.9
- conv_shift: float32 [1536], P('tp'), may hold values from -2.5 to 2.5
Outputs:
- attended: bfloat16 [24576, 1536], P(('dp', 'ctx', 'tp')), parts along dimension 0
- conv_out: bfloat16 [24576, 1536], P(('dp', 'ctx'), 'tp'), parts along dimension 0
There are 4 independent parts, one for each index of `dp`. A program takes and returns all parts, laid end to end along the dimension named above; an argument that names none is the same for every part. Nothing has to cross between parts.
All inputs are finite; a program needn't handle non-finite values.
Results may differ from a plain program's by a relative error of at most 0.008.
Values may be sent and summed in bfloat16 or wider, within the bound.
A program may use at most 64 MiB of HBM per device.

v0:
```python
import math

import jax
import jax.numpy as jnp
from jax import lax
from jax.sharding import PartitionSpec as P

KERNEL = 31
KEY_BLOCK = 64
HD = 96


def with_halo(cells, sides, width):
    for axis, dim in sides:
        count = lax.axis_size(axis)
        ends = count - 1
        head = lax.slice_in_dim(cells, 0, width, axis=dim)
        tail = lax.slice_in_dim(cells, cells.shape[dim] - width, cells.shape[dim], axis=dim)
        cells = jnp.concatenate(
            [
                lax.ppermute(tail, axis, [(i, (i + 1) % count) for i in range(ends)]),
                cells,
                lax.ppermute(head, axis, [((i + 1) % count, i) for i in range(ends)]),
            ],
            axis=dim,
        )
    return cells


def attend_rows(queries, carried, key_piece, value_piece):
    row_count = queries.shape[0]
    heads_here = queries.shape[1] // HD
    key_count = key_piece.shape[0]
    blocks = key_count // KEY_BLOCK
    per_step = math.gcd(blocks, 16)
    inv_root = 1.0 / math.sqrt(HD)
    query_heads = queries.reshape(row_count, heads_here, HD)
    key_groups = key_piece.reshape(blocks // per_step, per_step * KEY_BLOCK, heads_here, HD)
    value_groups = value_piece.reshape(blocks // per_step, per_step, KEY_BLOCK, heads_here, HD)

    def advance(current, paired):
        top_score, weight_sum, mixture = current
        key_rows, value_rows = paired
        scores = (
            jnp.einsum("thd,khd->htk", query_heads, key_rows, preferred_element_type=jnp.float32)
            * inv_root
        )
        scores = scores.reshape(heads_here, row_count, per_step, KEY_BLOCK)
        block_top = scores.max(-1)
        lifted = jnp.exp(scores - block_top[..., None])
        block_sums = lifted.sum(-1)
        weights = lifted.astype(jnp.bfloat16)
        block_mix = jnp.einsum(
            "htgk,gkhd->htgd", weights, value_rows, preferred_element_type=jnp.float32
        )
        new_top = jnp.maximum(top_score, block_top.max(-1))
        carry_scale = jnp.exp(top_score - new_top)
        block_scale = jnp.exp(block_top - new_top[..., None])
        weight_sum = weight_sum * carry_scale + (block_sums * block_scale).sum(-1)
        mixture = mixture * carry_scale[..., None] + (block_mix * block_scale[..., None]).sum(2)
        return ((new_top, weight_sum, mixture), None)

    final_state, unused = lax.scan(advance, carried, (key_groups, value_groups))
    return final_state


def layer_norm(source, norm_gain, norm_bias):
    rows_float = source.astype(jnp.float32)
    row_mean = rows_float.mean(-1, keepdims=True)
    centred = rows_float - row_mean
    row_var = (centred * centred).mean(-1, keepdims=True)
    return centred * lax.rsqrt(row_var + 1e-05) * norm_gain + norm_bias


def shards(
    residual_in,
    queries,
    keys,
    values,
    out_weight,
    norm_gain,
    norm_bias,
    glu_weight,
    conv_weight,
    conv_scale,
    conv_shift,
):
    row_count = queries.shape[0]
    heads_here = queries.shape[1] // HD
    initial = (
        jnp.full((heads_here, row_count), -1e30, jnp.float32),
        jnp.zeros((heads_here, row_count), jnp.float32),
        jnp.zeros((heads_here, row_count, HD), jnp.float32),
    )
    all_keys, all_values = (
        lax.all_gather(keys, "ctx", axis=0, tiled=True),
        lax.all_gather(values, "ctx", axis=0, tiled=True),
    )
    final_state = attend_rows(queries, initial, all_keys, all_values)
    mixture = final_state[2] / final_state[1][..., None]
    context = mixture.transpose(1, 0, 2).reshape(row_count, heads_here * HD).astype(jnp.bfloat16)
    own_count = row_count // lax.axis_size("tp")
    offset = lax.axis_index("tp") * own_count
    summed = lax.psum_scatter(
        jnp.dot(context, out_weight, preferred_element_type=jnp.float32),
        "tp",
        scatter_dimension=0,
        tiled=True,
    )
    own_rows = lax.dynamic_slice_in_dim(residual_in, offset, own_count, 0)
    attended = (own_rows.astype(jnp.float32) + summed).astype(jnp.bfloat16)
    own_normed = layer_norm(attended, norm_gain, norm_bias).astype(jnp.bfloat16)
    normed = lax.all_gather(own_normed, "tp", axis=0, tiled=True)
    local_width = glu_weight.shape[2]
    projection = glu_weight.reshape(glu_weight.shape[0], 2 * local_width)
    rim_width = (KERNEL - 1) // 2
    projected = jnp.dot(normed, projection, preferred_element_type=jnp.float32)
    padded = with_halo(
        (projected[:, :local_width] * jax.nn.sigmoid(projected[:, local_width:])).astype(
            jnp.bfloat16
        ),
        (("ctx", 0),),
        rim_width,
    )
    conv_sum = jnp.zeros((row_count, local_width), jnp.float32)
    for tap_index in range(KERNEL):
        conv_sum = (
            conv_sum
            + padded[tap_index : tap_index + row_count].astype(jnp.float32) * conv_weight[tap_index]
        )
    shifted = conv_sum * conv_scale + conv_shift
    conv_out = (shifted * jax.nn.sigmoid(shifted)).astype(jnp.bfloat16)
    return (attended, conv_out)


def solution(mesh):
    return jax.shard_map(
        shards,
        mesh=mesh,
        in_specs=(
            P(("dp", "ctx"), None),
            P(("dp", "ctx"), "tp"),
            P(("dp", "ctx"), "tp"),
            P(("dp", "ctx"), "tp"),
            P("tp", None),
            P(),
            P(),
            P(None, None, "tp"),
            P(None, "tp"),
            P("tp"),
            P("tp"),
        ),
        out_specs=(P(("dp", "ctx", "tp"), None), P(("dp", "ctx"), "tp")),
        check_vma=False,
    )
```

profile of v0, /device:TPU:30, one launch (start us, length us, event | category | flops | bytes accessed | tf_op | source)
XLA Modules:
  0.0 409.4 jit_solution(6169325109921796510)
XLA Ops:
  9.8 92.2 %all-gather.3.cloned.1.call-done = bf16[6144,384]{1,0:T(8,128)(2,1)} async-done(((bf16[192,384]{1,0:T(8,128)(2,1)}), bf16[6144,384]{1,0:T(8,128)(2,1)}) %all-gather.3.cloned.1.call-update) | async-done | bytes 4718608 | tf_op jit(solution)/shard_map/all_gather | solution.py:96
  102.1 12.4 %reshape.50 = bf16[6,1024,4,96]{3,2,1,0:T(4,128)(2,1)} reshape(bf16[6144,384]{1,0:T(8,128)(2,1)} %all-gather.3.cloned.1.call-done) | data formatting | bytes 9437184 | tf_op jit(solution)/shard_map/reshape | solution.py:38
  114.4 10.2 %copy.22 = bf16[6,1024,4,96]{1,3,2,0:T(8,128)(2,1)} copy(bf16[6,1024,4,96]{3,2,1,0:T(4,128)(2,1)} %reshape.50) | data formatting | bytes 9437184
  124.7 67.0 %all-gather.5.cloned.1.call-done = bf16[6144,384]{1,0:T(8,128)(2,1)} async-done(((bf16[192,384]{1,0:T(8,128)(2,1)}), bf16[6144,384]{1,0:T(8,128)(2,1)}) %all-gather.5.cloned.1.call-update) | async-done | bytes 4718608 | tf_op jit(solution)/shard_map/all_gather | solution.py:97
  191.7 12.4 %reshape.47 = bf16[6,16,64,4,96]{4,3,2,1,0:T(4,128)(2,1)} reshape(bf16[6144,384]{1,0:T(8,128)(2,1)} %all-gather.5.cloned.1.call-done) | data formatting | bytes 9437184 | tf_op jit(solution)/shard_map/reshape | solution.py:39
  204.0 110.3 %while.15 = (s32[]{:T(128)}, f32[4,192]{1,0:T(4,128)S(1)}, f32[4,192]{1,0:T(4,128)S(1)}, f32[4,192,96]{1,2,0:T(8,128)S(1)}, bf16[6,1024,4,96]{1,3,2,0:T(8,128)(2...) while((s32[]{:T(128)}, f32[4,192]{1,0:T(4,128)S(1)}, ...), condition=%wide.region_6.7_spmd.clone, body=%wide.region_0.6_spmd.clone.sunk | while | flops 310017792 | bytes 36370056 | solution.py:63
  204.0 3.3 fusion.68
  207.4 5.0 %copy.36 = f32[4,192,1024]{1,2,0:T(8,128)} copy(f32[4,192,1024]{2,1,0:T(8,128)} %get-tuple-element.185) | data formatting | bytes 6291456 | tf_op jit(solution)/shard_map/while/body/eval_jaxpr/mul | solution.py:45
  212.3 3.0 bitcast_reduce_fusion.2
  218.6 3.6 fusion.71
  222.4 3.3 fusion.68
  225.7 5.0 %copy.36 = f32[4,192,1024]{1,2,0:T(8,128)} copy(f32[4,192,1024]{2,1,0:T(8,128)} %get-tuple-element.185) | data formatting | bytes 6291456 | tf_op jit(solution)/shard_map/while/body/eval_jaxpr/mul | solution.py:45
  230.7 3.0 bitcast_reduce_fusion.2
  237.0 3.6 fusion.71
  240.8 3.3 fusion.68
  244.1 5.0 %copy.36 = f32[4,192,1024]{1,2,0:T(8,128)} copy(f32[4,192,1024]{2,1,0:T(8,128)} %get-tuple-element.185) | data formatting | bytes 6291456 | tf_op jit(solution)/shard_map/while/body/eval_jaxpr/mul | solution.py:45
  249.1 3.0 bitcast_reduce_fusion.2
  255.4 3.6 fusion.71
  259.2 3.3 fusion.68
  262.5 5.0 %copy.36 = f32[4,192,1024]{1,2,0:T(8,128)} copy(f32[4,192,1024]{2,1,0:T(8,128)} %get-tuple-element.185) | data formatting | bytes 6291456 | tf_op jit(solution)/shard_map/while/body/eval_jaxpr/mul | solution.py:45
  267.5 3.0 bitcast_reduce_fusion.2
  273.8 3.6 fusion.71
  277.6 3.3 fusion.68
  280.9 5.0 %copy.36 = f32[4,192,1024]{1,2,0:T(8,128)} copy(f32[4,192,1024]{2,1,0:T(8,128)} %get-tuple-element.185) | data formatting | bytes 6291456 | tf_op jit(solution)/shard_map/while/body/eval_jaxpr/mul | solution.py:45
  292.2 3.6 fusion.71
  295.9 3.3 fusion.68
  299.3 5.0 %copy.36 = f32[4,192,1024]{1,2,0:T(8,128)} copy(f32[4,192,1024]{2,1,0:T(8,128)} %get-tuple-element.185) | data formatting | bytes 6291456 | tf_op jit(solution)/shard_map/while/body/eval_jaxpr/mul | solution.py:45
  310.6 3.6 fusion.71
  319.6 49.1 %reduce-scatter.2.cloned.1.call-done = f32[48,1536]{1,0:T(8,128)} async-done(((f32[192,1536]{1,0:T(8,128)}), f32[48,1536]{1,0:T(8,128)}) %reduce-scatter.2.cloned.1.call-update) | async-done | bytes 294928 | tf_op jit(solution)/shard_map/reduce_scatter | solution.py:104
  370.3 13.7 %all_gather.11 = bf16[192,1536]{1,0:T(8,128)(2,1)S(1)} all-gather(bf16[48,1536]{1,0:T(8,128)(2,1)S(1)} %fusion.16), channel_id=1, replica_groups=mesh['dp'=4,'ctx'=32,'tp'=4] {'tp'}, dimensions={0}, use_global_device_ids=true | all-gather | bytes 737280 | tf_op jit(solution)/shard_map/all_gather | solution.py:113
  386.4 4.6 %collective-permute-start = (bf16[15,384]{1,0:T(8,128)(2,1)S(1)}, bf16[15,384]{1,0:T(8,128)(2,1)S(1)}, u32[]{:S(2)}, u32[]{:S(2)}) collective-permute-start(bf16[15,384]{1,0:T(8,128)(2,1)S(1)} %get-tuple-element.133), channel_id=1, source_target_pairs={{0,4},{4,8},{8,12},{12,16},{16,20},{20,24},{24,28},{28,32},{32,36}... | collective-permute-start | bytes 34568 | tf_op jit(solution)/shard_map/ppermute | solution.py:21
  394.0 5.9 %collective-permute-done.1 = bf16[15,384]{1,0:T(8,128)(2,1)S(1)} collective-permute-done((bf16[15,384]{1,0:T(8,128)(2,1)S(1)}, bf16[15,384]{1,0:T(8,128)(2,1)S(1)}, u32[]{:S(2)}, u32[]{:S(2)}) %collective-permute-start.1) | collective-permute-done | bytes 11552 | tf_op jit(solution)/shard_map/ppermute | solution.py:23
  (97 shorter events, 44.0 us)
Async XLA Ops:
  7.2 307.2 %copy-start = (bf16[384,1536]{1,0:T(8,128)(2,1)S(1)}, bf16[384,1536]{1,0:T(8,128)(2,1)}, u32[]{:S(2)}) copy-start(bf16[384,1536]{1,0:T(8,128)(2,1)} %param.17) | copy-start | bytes 3538948
  7.2 94.9 %all-gather.3.cloned.1.call-start = ((), (), s32[]{:S(2)}) async-start(), calls=%async_computation.1 | async-start | bytes 4866048 | tf_op jit(solution)/shard_map/all_gather | solution.py:96
  7.9 183.8 %all-gather.5.cloned.1.call-start = ((), (), s32[]{:S(2)}) async-start(), calls=%async_computation.2 | async-start | bytes 4866048 | tf_op jit(solution)/shard_map/all_gather | solution.py:97
  8.7 360.1 %reduce-scatter.2.cloned.1.call-start = ((), (), s32[]{:S(2)}) async-start(), calls=%async_computation.3 | async-start | bytes 1474560 | tf_op jit(solution)/shard_map/reduce_scatter | solution.py:104
  212.3 3.4 copy-start.1
  230.7 3.4 copy-start.1
  249.1 3.4 copy-start.1
  267.5 3.4 copy-start.1
  285.9 3.4 copy-start.1
  304.3 3.4 copy-start.1
  314.4 2.0 copy-start.2
  314.4 55.8 %copy-start.4 = (f32[1536]{0:T(1024)S(1)}, f32[1536]{0:T(1024)}, u32[]{:S(2)}) copy-start(f32[1536]{0:T(1024)} %param.19) | copy-start | bytes 18436
  314.4 55.8 %copy-start.5 = (f32[1536]{0:T(1024)S(1)}, f32[1536]{0:T(1024)}, u32[]{:S(2)}) copy-start(f32[1536]{0:T(1024)} %param.18) | copy-start | bytes 18436
  318.3 81.6 %copy-start.6 = (f32[384]{0:T(512)S(1)}, f32[384]{0:T(512)}, u32[]{:S(2)}) copy-start(f32[384]{0:T(512)} %param.23) | copy-start | bytes 4612
  318.3 81.6 %copy-start.7 = (f32[384]{0:T(512)S(1)}, f32[384]{0:T(512)}, u32[]{:S(2)}) copy-start(f32[384]{0:T(512)} %param.22) | copy-start | bytes 4612
  369.9 32.9 %copy-start.3 = (bf16[48,1536]{1,0:T(8,128)(2,1)}, bf16[48,1536]{1,0:T(8,128)(2,1)S(1)}, u32[]{:S(2)}) copy-start(bf16[48,1536]{1,0:T(8,128)(2,1)S(1)} %get-tuple-element.130) | copy-start | bytes 442372
  386.4 7.6 %collective-permute-start = (bf16[15,384]{1,0:T(8,128)(2,1)S(1)}, bf16[15,384]{1,0:T(8,128)(2,1)S(1)}, u32[]{:S(2)}, u32[]{:S(2)}) collective-permute-start(bf16[15,384]{1,0:T(8,128)(2,1)S(1)} %get-tuple-element.133), channel_id=1, source_target_pairs={{0,4},{4,8},{8,12},{12,16},{16,20},{20,24},{24,28},{28,32},{32,36}... | collective-permute-start | bytes 34568 | tf_op jit(solution)/shard_map/ppermute | solution.py:21
  391.0 8.9 %collective-permute-start.1 = (bf16[15,384]{1,0:T(8,128)(2,1)S(1)}, bf16[15,384]{1,0:T(8,128)(2,1)S(1)}, u32[]{:S(2)}, u32[]{:S(2)}) collective-permute-start(bf16[15,384]{1,0:T(8,128)(2,1)S(1)} %get-tuple-element.134), channel_id=1, source_target_pairs={{4,0},{8,4},{12,8},{16,12},{20,16},{24,20},{28,24},{32,28},{36,32}... | collective-permute-start | bytes 34568 | tf_op jit(solution)/shard_map/ppermute | solution.py:23
Sparse Core Ops, SparseCore 0:
  11.2 90.8 all-gather.2
  105.2 86.3 all-gather.4
  316.1 52.6 reduce-scatter.1
where the time goes:
time: 412 us; the launch traced here: 409 us
  waiting for transfers between devices  216 us (52%)
  local copies, waits for them, and re-layouts  82.9 us (20%)
  matrix products  45.3 us (11%)
  other arithmetic  30.9 us (8%)
  between operations  13.9 us (3%)
  blocking collectives  13.7 us (3%)
  starting transfers between devices  6.62 us (2%)
    all_gather x1, waiting for transfers between devices, shards(): lax.all_gather(keys, 'ctx', axis=0, tiled=True)  92.2 us
    all_gather x1, waiting for transfers between devices, shards(): lax.all_gather(values, 'ctx', axis=0, tiled=True)  67 us
    reduce_scatter x1, waiting for transfers between devices, shards(): lax.psum_scatter(jnp.dot(context, out_weight, preferred_element_type=jnp....  49.1 us
    mul x6, local copies, waits for them, and re-layouts, advance(): jnp.einsum('thd,khd->htk', query_heads, key_rows, preferred_element_type=...  29.9 us
    dot_general x6, matrix products, advance(): jnp.einsum('htgk,gkhd->htgd', weights, value_rows, preferred_element_type...  21.5 us
    dot_general x6, matrix products, advance(): jnp.einsum('thd,khd->htk', query_heads, key_rows, preferred_element_type=...  20 us
    reduce_max x6, other arithmetic, advance(): block_top = scores.max(-1)  18.2 us
    all_gather x1, blocking collectives, shards(): normed = lax.all_gather(own_normed, 'tp', axis=0, tiled=True)  13.7 us
  transfers between devices with their start and end apart: 5, of which 4 were waited for; matrix products, arithmetic and copies ran while one was open for 7% of the time, Pallas kernels for 0%

commit v1 on v0

v1 whole, which is shorter than its diff:
```python
import functools
import math

import jax
import jax.numpy as jnp
from jax import lax
from jax.experimental import pallas as pl
from jax.experimental.pallas import tpu as pltpu
from jax.sharding import PartitionSpec as P

KERNEL = 31
HD = 96
LANES = 128
MESH = pl.DeviceIdType.MESH
F32 = jnp.float32
BF16 = jnp.bfloat16


def wait_for(ref, sem):
    pltpu.make_async_copy(ref, ref, sem).wait()


def send(src, dst, send_sem, recv_sem, device):
    pltpu.make_async_remote_copy(
        src_ref=src,
        dst_ref=dst,
        send_sem=send_sem,
        recv_sem=recv_sem,
        device_id=device,
        device_id_type=MESH,
    ).start()


def send_or_keep(here, src, dst, send_sem, recv_sem, device):
    @pl.when(here)
    def _():
        pltpu.make_async_copy(src, dst, recv_sem).start()

    @pl.when(jnp.logical_not(here))
    def _():
        send(src, dst, send_sem, recv_sem, device)


def kernel(
    ny,
    nx,
    resid_ref,
    q_ref,
    k_ref,
    v_ref,
    w_ref,
    gain_ref,
    bias_ref,
    glu_ref,
    taps_ref,
    scale_ref,
    shift_ref,
    att_ref,
    conv_ref,
    qs,
    kvs,
    qbuf,
    kvbuf,
    qfull,
    vfull,
    top,
    acc,
    accr,
    ctxs,
    cbuf,
    cat,
    wall,
    gw,
    resid,
    own,
    zs,
    zr,
    nbuf,
    gpad,
    hs,
    hr,
    sq_s,
    skv_s,
    q_r,
    qf_s,
    kv_r,
    xr_s,
    xl_s,
    xf_s,
    a_s,
    a_r,
    c_s,
    c_r,
    w_s,
    w_r,
    l_r,
    z_s,
    z_r,
    nz_s,
    ns_s,
    nf_s,
    n_r,
    h_s,
    h_r,
):
    half = ny // 2
    rows = q_ref.shape[0]
    block = rows // 4
    rim = gpad.shape[0] - rows
    rim = rim // 2
    width = conv_ref.shape[1]
    dp = lax.axis_index("dp")
    ctx = lax.axis_index("ctx")
    tp = lax.axis_index("tp")
    n_ctx = ny * nx
    y, x = ctx // nx, ctx % nx
    zh, core = tp // 2, tp % 2
    parity = y % 2

    def dev(yy, xx, tt):
        return (dp, yy * nx + xx, tt)

    sibling = (dp, ctx, zh * 2 + 1 - core)
    partner = (dp, ctx, (1 - zh) * 2 + core)
    x_right, x_left, x_far = (x + 1) % nx, (x + nx - 1) % nx, (x + 2) % nx
    right, left = dev(y, x_right, tp), dev(y, x_left, tp)

    barrier = pltpu.get_barrier_semaphore()

    def greet(device):
        pl.semaphore_signal(barrier, inc=1, device_id=device, device_id_type=MESH)

    for o in range(1, ny):
        for cc in range(2):
            greet(dev((y + o) % ny, x, zh * 2 + cc))
    greet(sibling)
    greet(partner)
    greet(right)
    greet(left)
    greet((dp, (ctx + 1) % n_ctx, tp))
    greet((dp, (ctx + n_ctx - 1) % n_ctx, tp))

    own_w = pltpu.make_async_copy(w_ref, wall.at[core], l_r.at[0])
    own_w.start()
    own_g = pltpu.make_async_copy(glu_ref, gw, l_r.at[1])
    own_g.start()
    own_x = pltpu.make_async_copy(
        resid_ref.at[pl.ds(pl.multiple_of(tp * block, block), block)], resid, l_r.at[2]
    )
    own_x.start()

    cut = rows * 3 // 4
    part = rows - cut
    for j in range(half):
        lo = HD * j
        kvs[j, 0:rows] = jnp.concatenate(
            [k_ref[:, lo : lo + HD], v_ref[:, lo : lo + 32]], axis=1
        )
        kvs[j, rows : rows + rows // 2] = jnp.concatenate(
            [v_ref[0 : rows // 2, lo + 32 : lo + HD], v_ref[rows // 2 : rows, lo + 32 : lo + HD]],
            axis=1,
        )
        qs[j] = jnp.concatenate(
            [
                q_ref[0:cut, lo : lo + HD],
                jnp.concatenate(
                    [q_ref[cut:rows, lo + 32 * i : lo + 32 * (i + 1)] for i in range(3)], axis=0
                ),
            ],
            axis=1,
        )

    pl.semaphore_wait(barrier, 2 * (ny - 1) + 6)

    for i in range(half):
        j = (y + i) % half
        head = core * half + j
        here = jnp.logical_and(head == y, core == parity)
        send_or_keep(
            here, qs.at[j], qbuf.at[y], sq_s.at[j], q_r.at[y], dev(head, x, zh * 2 + parity)
        )
    for i in range(half):
        j = (y + i) % half
        head = core * half + j
        here = jnp.logical_and(head == y, core == parity)
        send_or_keep(
            here,
            kvs.at[j],
            kvbuf.at[x, y // 2],
            skv_s.at[j],
            kv_r.at[x, y // 2],
            dev(head, x, zh * 2 + parity),
        )

    for i in range(half):
        ys = 2 * ((y // 2 + i) % half) + core
        wait_for(qbuf.at[ys], q_r.at[ys])
        send(qbuf.at[ys], qbuf.at[ys], qf_s.at[i], q_r.at[ys], sibling)
    for i in range(half):
        s = (y // 2 + i) % half
        wait_for(kvbuf.at[x, s], kv_r.at[x, s])
        send(kvbuf.at[x, s], kvbuf.at[x, s], xr_s.at[s], kv_r.at[x, s], right)
        send(kvbuf.at[x, s], kvbuf.at[x, s], xl_s.at[s], kv_r.at[x, s], left)
    send(w_ref, wall.at[core], w_s, w_r, sibling)
    for i in range(half):
        ys = 2 * ((y // 2 + i) % half) + 1 - core
        wait_for(qbuf.at[ys], q_r.at[ys])

    @pl.loop(0, ny)
    def _(t):
        base = pl.multiple_of(t * rows, rows)
        qfull[pl.ds(base, cut)] = jnp.concatenate(
            [qbuf[t, :, 0:HD], jnp.zeros((cut, LANES - HD), BF16)], axis=1
        )
        qfull[pl.ds(base + cut, part)] = jnp.concatenate(
            [qbuf[t, part * i : part * (i + 1), HD:LANES] for i in range(3)]
            + [jnp.zeros((part, LANES - HD), BF16)],
            axis=1,
        )

    factor = math.log2(math.e) / math.sqrt(HD)
    hr_rows = rows // 2
    keys = half * rows

    def unpack(slot):
        @pl.loop(0, half)
        def _(s):
            base = pl.multiple_of(s * rows, rows)
            ones = jnp.ones((hr_rows, LANES - HD), BF16)
            for b in range(2):
                vfull[pl.ds(base + b * hr_rows, hr_rows)] = jnp.concatenate(
                    [
                        kvbuf[slot, s, b * hr_rows : (b + 1) * hr_rows, HD:LANES],
                        kvbuf[slot, s, rows : rows + hr_rows, 64 * b : 64 * (b + 1)],
                        ones,
                    ],
                    axis=1,
                )

    def tile(slot, t, first):
        at = pl.ds(pl.multiple_of(t * rows, rows), rows)
        kk = kvbuf[slot, :, 0:rows, :].reshape(keys, LANES)
        s = lax.dot_general(
            qfull[at], kk, (((1,), (1,)), ((), ())), preferred_element_type=F32
        )
        peak = jnp.max(s, axis=1, keepdims=True) * factor
        if first:
            new = peak
        else:
            old = top[at][:, 0:1]
            new = jnp.maximum(old, peak)
        p = jnp.exp2(s * factor - new)
        mix = jnp.dot(p.astype(BF16), vfull[...], preferred_element_type=F32)
        if not first:
            mix = mix + acc[at] * jnp.exp2(old - new)
        return at, mix, new

    def attend(slot, first):
        unpack(slot)

        @pl.loop(0, ny)
        def _(t):
            at, mix, new = tile(slot, t, first)
            acc[at] = mix
            top[at] = jnp.broadcast_to(new, (rows, LANES))

    attend(x, True)
    for s in range(half):
        wait_for(kvbuf.at[x_left, s], kv_r.at[x_left, s])
        if s < half // 2:
            send(kvbuf.at[x_left, s], kvbuf.at[x_left, s], xf_s.at[s], kv_r.at[x_left, s], right)
    for s in range(half // 2, half):
        wait_for(kvbuf.at[x_right, s], kv_r.at[x_right, s])
        send(kvbuf.at[x_right, s], kvbuf.at[x_right, s], xf_s.at[s], kv_r.at[x_right, s], left)
    attend(x_left, False)
    for s in range(half // 2):
        wait_for(kvbuf.at[x_right, s], kv_r.at[x_right, s])
    attend(x_right, False)
    for s in range(half):
        wait_for(kvbuf.at[x_far, s], kv_r.at[x_far, s])
    unpack(x_far)
    lane = lax.broadcasted_iota(jnp.int32, (rows, LANES), 1)

    @pl.loop(0, half)
    def _(k):
        at, mix, new = tile(x_far, (1 - core) * half + k, False)
        acc[at] = jnp.where(lane >= LANES - 16, jnp.broadcast_to(new, (rows, LANES)), mix)
        send(acc.at[at], accr.at[k], a_s.at[k], a_r.at[k], sibling)

    @pl.loop(0, half)
    def _(k):
        at, mix, new = tile(x_far, core * half + k, False)
        wait_for(accr.at[k], a_r.at[k])
        other = accr[k]
        other_top = other[:, LANES - 1 : LANES]
        both = jnp.maximum(new, other_top)
        total = mix * jnp.exp2(new - both) + other * jnp.exp2(other_top - both)
        out = (total / total[:, HD : HD + 1]).astype(BF16)
        for cc in range(2):
            for zz in range(2):
                src = (zz * 2 + cc) * block
                ctxs[k, cc, zz * block : (zz + 1) * block] = out[src : src + block]
        yd = core * half + k
        for cc in range(2):
            send_or_keep(
                jnp.logical_and(yd == y, core == cc),
                ctxs.at[k, cc],
                cbuf.at[y],
                c_s.at[k, cc],
                c_r.at[y],
                dev(yd, x, zh * 2 + cc),
            )

    own_w.wait()
    own_x.wait()
    wait_for(wall.at[1 - core], w_r)
    for h in range(ny):
        wait_for(cbuf.at[h], c_r.at[h])
        cat[:, HD * h : HD * (h + 1)] = cbuf[h, :, 0:HD]

    def project(zz):
        return jnp.dot(
            cat[pl.ds(pl.multiple_of(zz * block, block), block)],
            wall[...].reshape(wall.shape[0] * wall.shape[1], wall.shape[2]),
            preferred_element_type=F32,
        )

    pieces = z_s.shape[0]
    step = block // pieces
    zs[...] = project(1 - zh).astype(BF16)
    for i in range(pieces):
        send(
            zs.at[pl.ds(i * step, step)],
            zr.at[pl.ds(i * step, step)],
            z_s.at[i],
            z_r.at[i],
            partner,
        )
    own[...] = project(zh) + resid[...].astype(F32)
    for i in range(pieces):
        piece = pl.ds(i * step, step)
        wait_for(zr.at[piece], z_r.at[i])
        attended = (own[piece] + zr[piece].astype(F32)).astype(BF16)
        att_ref[piece] = attended
        full = attended.astype(F32)
        centred = full - jnp.mean(full, axis=1, keepdims=True)
        var = jnp.mean(centred * centred, axis=1, keepdims=True)
        normed = centred * lax.rsqrt(var + 1e-05) * gain_ref[...].reshape(1, -1)
        nbuf[tp, piece] = (normed + bias_ref[...].reshape(1, -1)).astype(BF16)
        send(nbuf.at[tp, piece], nbuf.at[tp, piece], nz_s.at[i], n_r.at[tp, i], partner)
        send(nbuf.at[tp, piece], nbuf.at[tp, piece], ns_s.at[i], n_r.at[tp, i], sibling)

    def gate(zz):
        data = nbuf[pl.ds(zz * 2, 2)].reshape(2 * block, nbuf.shape[2])
        projected = jnp.dot(data, gw[...], preferred_element_type=F32)
        gated = projected[:, 0:width] * jax.nn.sigmoid(projected[:, width:])
        base = pl.multiple_of(rim + zz * 2 * block, 16)
        gpad[pl.ds(base, 2 * block)] = gated.astype(BF16).astype(F32)
        edge = pl.multiple_of(rim + zz * (rows - rim), 16)
        hs[zz] = gpad[pl.ds(edge, rim)].astype(BF16)
        target = ctx + 2 * zz - 1

        @pl.when(jnp.logical_and(target >= 0, target < n_ctx))
        def _():
            send(hs.at[zz], hr.at[1 - zz], h_s.at[zz], h_r.at[1 - zz], (dp, target, tp))

    own_g.wait()
    for i in range(pieces):
        wait_for(
            nbuf.at[zh * 2 + 1 - core, pl.ds(i * step, step)], n_r.at[zh * 2 + 1 - core, i]
        )
    gate(zh)
    tp_other = (1 - zh) * 2 + core
    for i in range(pieces):
        piece = pl.ds(i * step, step)
        wait_for(nbuf.at[tp_other, piece], n_r.at[tp_other, i])
        send(
            nbuf.at[tp_other, piece],
            nbuf.at[tp_other, piece],
            nf_s.at[i],
            n_r.at[tp_other, i],
            sibling,
        )
    for i in range(pieces):
        tp_last = (1 - zh) * 2 + 1 - core
        wait_for(nbuf.at[tp_last, pl.ds(i * step, step)], n_r.at[tp_last, i])
    gate(1 - zh)

    for side in range(2):
        source = ctx + 2 * side - 1
        exists = jnp.logical_and(source >= 0, source < n_ctx)
        place = pl.ds(side * (rim + rows), rim)

        @pl.when(exists)
        def _():
            wait_for(hr.at[side], h_r.at[side])
            gpad[place] = hr[side].astype(F32)

        @pl.when(jnp.logical_not(exists))
        def _():
            gpad[place] = jnp.zeros((rim, width), F32)

    offset = rim - (KERNEL - 1) // 2
    tall = 2 * rim
    taps = taps_ref[...]
    scale = scale_ref[...].reshape(1, -1)
    shift = shift_ref[...].reshape(1, -1)

    @pl.loop(0, rows // rim)
    def _(r):
        at = pl.multiple_of(r * rim, rim)
        window = gpad[pl.ds(at, rim + tall)]
        total = window[offset : offset + rim] * taps[0:1]
        for k in range(1, KERNEL):
            total = total + window[offset + k : offset + k + rim] * taps[k : k + 1]
        u = total * scale + shift
        conv_ref[pl.ds(at, rim)] = (u * jax.nn.sigmoid(u)).astype(BF16)

    for j in range(half):
        here = jnp.logical_and(core * half + j == y, core == parity)

        @pl.when(jnp.logical_not(here))
        def _():
            wait_for(qs.at[j], sq_s.at[j])
            wait_for(kvs.at[j], skv_s.at[j])

        wait_for(qbuf.at[j], qf_s.at[j])
        wait_for(kvbuf.at[x, j], xr_s.at[j])
        wait_for(kvbuf.at[x, j], xl_s.at[j])
        wait_for(kvbuf.at[x, j], xf_s.at[j])
        wait_for(accr.at[j], a_s.at[j])
        for cc in range(2):

            @pl.when(jnp.logical_not(jnp.logical_and(core * half + j == y, core == cc)))
            def _():
                wait_for(ctxs.at[j, cc], c_s.at[j, cc])

    wait_for(wall.at[core], w_s)
    for i in range(pieces):
        piece = pl.ds(i * step, step)
        wait_for(zs.at[piece], z_s.at[i])
        wait_for(nbuf.at[tp, piece], nz_s.at[i])
        wait_for(nbuf.at[tp, piece], ns_s.at[i])
        wait_for(nbuf.at[tp_other, piece], nf_s.at[i])
    for side in range(2):
        target = ctx + 2 * side - 1

        @pl.when(jnp.logical_and(target >= 0, target < n_ctx))
        def _():
            wait_for(hs.at[side], h_s.at[side])


def shards(
    n_ctx,
    residual_in,
    queries,
    keys,
    values,
    out_weight,
    norm_gain,
    norm_bias,
    glu_weight,
    conv_weight,
    conv_scale,
    conv_shift,
):
    rows, columns = queries.shape
    half = columns // HD
    ny = 2 * half
    nx = n_ctx // ny
    model = residual_in.shape[1]
    block = rows // 4
    pieces = block // 16
    rim = 16
    vmem = pl.BlockSpec(memory_space=pltpu.VMEM)
    anywhere = pl.BlockSpec(memory_space=pl.ANY)
    dma = pltpu.SemaphoreType.DMA
    tall = rows + rows // 2
    scratch = [
        pltpu.VMEM((half, rows * 3 // 4, LANES), BF16),
        pltpu.VMEM((half, tall, LANES), BF16),
        pltpu.VMEM((ny, rows * 3 // 4, LANES), BF16),
        pltpu.VMEM((nx, half, tall, LANES), BF16),
        pltpu.VMEM((ny * rows, LANES), BF16),
        pltpu.VMEM((half * rows, LANES), BF16),
        pltpu.VMEM((ny * rows, LANES), F32),
        pltpu.VMEM((ny * rows, LANES), F32),
        pltpu.VMEM((half, rows, LANES), F32),
        pltpu.VMEM((half, 2, 2 * block, LANES), BF16),
        pltpu.VMEM((ny, 2 * block, LANES), BF16),
        pltpu.VMEM((2 * block, ny * HD), BF16),
        pltpu.VMEM((2, half * HD, model), BF16),
        pltpu.VMEM((model, 2 * columns), BF16),
        pltpu.VMEM((block, model), BF16),
        pltpu.VMEM((block, model), F32),
        pltpu.VMEM((block, model), BF16),
        pltpu.VMEM((block, model), BF16),
        pltpu.VMEM((4, block, model), BF16),
        pltpu.VMEM((rows + 2 * rim, columns), F32),
        pltpu.VMEM((2, rim, columns), BF16),
        pltpu.VMEM((2, rim, columns), BF16),
        dma((half,)),
        dma((half,)),
        dma((ny,)),
        dma((half,)),
        dma((nx, half)),
        dma((half,)),
        dma((half,)),
        dma((half,)),
        dma((half,)),
        dma((half,)),
        dma((half, 2)),
        dma((ny,)),
        dma,
        dma,
        dma((3,)),
        dma((pieces,)),
        dma((pieces,)),
        dma((pieces,)),
        dma((pieces,)),
        dma((pieces,)),
        dma((4, pieces)),
        dma((2,)),
        dma((2,)),
    ]
    return pl.pallas_call(
        functools.partial(kernel, ny, nx),
        out_shape=(
            jax.ShapeDtypeStruct((block, model), BF16),
            jax.ShapeDtypeStruct((rows, columns), BF16),
        ),
        in_specs=[anywhere, vmem, vmem, vmem, anywhere, vmem, vmem, anywhere, vmem, vmem, vmem],
        out_specs=(vmem, vmem),
        scratch_shapes=scratch,
        compiler_params=pltpu.CompilerParams(
            collective_id=0, has_side_effects=True, vmem_limit_bytes=56 * 1024 * 1024
        ),
        cost_estimate=pl.CostEstimate(
            flops=3 * 10**9, bytes_accessed=10**7, transcendentals=5 * 10**6
        ),
    )(
        residual_in,
        queries,
        keys,
        values,
        out_weight,
        norm_gain,
        norm_bias,
        glu_weight.reshape(glu_weight.shape[0], 2 * columns),
        conv_weight,
        conv_scale,
        conv_shift,
    )


def solution(mesh):
    return jax.shard_map(
        functools.partial(shards, mesh.shape["ctx"]),
        mesh=mesh,
        in_specs=(
            P(("dp", "ctx"), None),
            P(("dp", "ctx"), "tp"),
            P(("dp", "ctx"), "tp"),
            P(("dp", "ctx"), "tp"),
            P("tp", None),
            P(),
            P(),
            P(None, None, "tp"),
            P(None, "tp"),
            P("tp"),
            P("tp"),
        ),
        out_specs=(P(("dp", "ctx", "tp"), None), P(("dp", "ctx"), "tp")),
        check_vma=False,
    )
```

time: 412 us -> 87.7 us (0.21)
  the two profiles are of different devices: /device:TPU:30 before, /device:TPU:137 now
where the time goes in v1:
time: 87.7 us; the launch traced here: 87.3 us
  Pallas kernels  80 us (91%)
  local copies, waits for them, and re-layouts  6.71 us (8%)
    pallas_call x1, Pallas kernels, shards(): pl.pallas_call(functools.partial(kernel, ny, nx), out_shape=(jax.ShapeDty...  80 us
    unnamed x3, local copies, waits for them, and re-layouts  6.71 us

profile of v1, /device:TPU:137, one launch (start us, length us, event | category | flops | bytes accessed | tf_op | source)
XLA Modules:
  0.0 87.3 jit_solution(9826550883483276734)
XLA Ops:
  0.6 3.5 %copy.13 = bf16[192,8,2,384]{3,1,2,0:T(8,128)(2,1)} copy(bf16[192,8,2,384]{3,2,1,0:T(2,128)(2,1)} %bitcast.2) | data formatting | bytes 4718592
  4.2 80.0 %shard_map.122 = (bf16[48,1536]{1,0:T(8,128)(2,1)}, bf16[192,384]{1,0:T(8,128)(2,1)}) custom-call(bf16[192,1536]{1,0:T(8,128)(2,1)} %resid_ref.1, bf16[192,384]{1,0:T(8,128)(2,1)} %q_ref.1, bf16[192,384]{1,0:T(8,128)(2,1)} %k_ref.1, bf16[192,384]{1,0:T(8,128)(2,1)} %v_ref.1, bf16[384,1536]{1,0:T(8,128)(2,1)} %w_ref.1, f32[1536]{0:T(1024)} %gain_ref.1, ...), custom_call_target="tpu_custom_call" | custom-call | flops 3000000000 | bytes 10000000 | tf_op jit(solution)/shard_map/pallas_call | solution.py:526
  84.2 1.6 %copy.16 = bf16[48,1536]{1,0:T(8,128)(2,1)} copy(bf16[48,1536]{1,0:T(8,128)(2,1)} %get-tuple-element.4) | data formatting | bytes 294912
  85.8 1.6 %copy.17 = bf16[192,384]{1,0:T(8,128)(2,1)} copy(bf16[192,384]{1,0:T(8,128)(2,1)} %get-tuple-element.5) | data formatting | bytes 294912

commit v2 on v1

--- a/solution.py
+++ b/solution.py
@@ -52,11 +52,8 @@
     gain_ref,
     bias_ref,
     glu_ref,
-    taps_ref,
-    scale_ref,
-    shift_ref,
     att_ref,
-    conv_ref,
+    gpad,
     qs,
     kvs,
     qbuf,
@@ -70,13 +67,13 @@
     cbuf,
     cat,
     wall,
+    graw,
     gw,
     resid,
     own,
     zs,
     zr,
     nbuf,
-    gpad,
     hs,
     hr,
     sq_s,
@@ -108,7 +105,7 @@
     block = rows // 4
     rim = gpad.shape[0] - rows
     rim = rim // 2
-    width = conv_ref.shape[1]
+    width = gpad.shape[1]
     dp = lax.axis_index("dp")
     ctx = lax.axis_index("ctx")
     tp = lax.axis_index("tp")
@@ -142,7 +139,7 @@
 
     own_w = pltpu.make_async_copy(w_ref, wall.at[core], l_r.at[0])
     own_w.start()
-    own_g = pltpu.make_async_copy(glu_ref, gw, l_r.at[1])
+    own_g = pltpu.make_async_copy(glu_ref, graw, l_r.at[1])
     own_g.start()
     own_x = pltpu.make_async_copy(
         resid_ref.at[pl.ds(pl.multiple_of(tp * block, block), block)], resid, l_r.at[2]
@@ -172,36 +169,71 @@
 
     pl.semaphore_wait(barrier, 2 * (ny - 1) + 6)
 
+    def rank(distance):
+        sign = distance // (half + 1)
+        fold = distance + sign * (ny - 2 * distance)
+        odd = distance % 2
+        return odd * (fold // 2 * 2 + sign) + (1 - odd) * (fold // 2 + fold // half + sign)
+
+    near = [0]
+    for o in range(1, half):
+        near += [o, ny - o]
+    near.append(half)
+
+    def to_head(o, src, dst, send_sem, recv_sem):
+        head = (y + o) % ny
+        j = head % half
+        device = dev(head, x, zh * 2 + parity)
+
+        @pl.when(head // half == core)
+        def _():
+            if o == 0:
+                send_or_keep(core == parity, src.at[j], dst, send_sem.at[j], recv_sem, device)
+            else:
+                send(src.at[j], dst, send_sem.at[j], recv_sem, device)
+
+    for o in near[::-1]:
+        to_head(o, qs, qbuf.at[y], sq_s, q_r.at[y])
+    for o in near:
+        place = rank((ny - o) % ny)
+        to_head(o, kvs, kvbuf.at[x, place], skv_s, kv_r.at[x, place])
+
     for i in range(half):
-        j = (y + i) % half
-        head = core * half + j
-        here = jnp.logical_and(head == y, core == parity)
-        send_or_keep(
-            here, qs.at[j], qbuf.at[y], sq_s.at[j], q_r.at[y], dev(head, x, zh * 2 + parity)
-        )
-    for i in range(half):
-        j = (y + i) % half
-        head = core * half + j
-        here = jnp.logical_and(head == y, core == parity)
-        send_or_keep(
-            here,
-            kvs.at[j],
-            kvbuf.at[x, y // 2],
-            skv_s.at[j],
-            kv_r.at[x, y // 2],
-            dev(head, x, zh * 2 + parity),
-        )
-
-    for i in range(half):
-        ys = 2 * ((y // 2 + i) % half) + core
+        ys = 2 * ((y // 2 + i + 1) % half) + core
         wait_for(qbuf.at[ys], q_r.at[ys])
         send(qbuf.at[ys], qbuf.at[ys], qf_s.at[i], q_r.at[ys], sibling)
-    for i in range(half):
-        s = (y // 2 + i) % half
+    send(w_ref, wall.at[core], w_s, w_r, sibling)
+    own_g.wait()
+    span = graw.shape[0] // half
+
+    def spread(s):
         wait_for(kvbuf.at[x, s], kv_r.at[x, s])
         send(kvbuf.at[x, s], kvbuf.at[x, s], xr_s.at[s], kv_r.at[x, s], right)
         send(kvbuf.at[x, s], kvbuf.at[x, s], xl_s.at[s], kv_r.at[x, s], left)
-    send(w_ref, wall.at[core], w_s, w_r, sibling)
+
+    def pass_on(s):
+        slot, target = (x_left, right) if s % 2 == 0 else (x_right, left)
+        wait_for(kvbuf.at[slot, s], kv_r.at[slot, s])
+        send(kvbuf.at[slot, s], kvbuf.at[slot, s], xf_s.at[s], kv_r.at[slot, s], target)
+
+    def arrive(slot, s):
+        wait_for(kvbuf.at[slot, s], kv_r.at[slot, s])
+
+    def relayout(i):
+        @pl.loop(0, span // 16)
+        def _(r):
+            at = pl.ds(pl.multiple_of(i * span + r * 16, 16), 16)
+            pair = graw[at].astype(F32)
+            gw[at] = jnp.concatenate([pair[:, 0, :], pair[:, 1, :]], axis=1).astype(BF16)
+
+    spread(0)
+    relayout(0)
+    spread(1)
+    relayout(1)
+    relayout(2)
+    pass_on(0)
+    relayout(3)
+    pass_on(1)
     for i in range(half):
         ys = 2 * ((y // 2 + i) % half) + 1 - core
         wait_for(qbuf.at[ys], q_r.at[ys])
@@ -220,26 +252,36 @@
 
     factor = math.log2(math.e) / math.sqrt(HD)
     hr_rows = rows // 2
-    keys = half * rows
-
-    def unpack(slot):
-        @pl.loop(0, half)
-        def _(s):
-            base = pl.multiple_of(s * rows, rows)
-            ones = jnp.ones((hr_rows, LANES - HD), BF16)
-            for b in range(2):
-                vfull[pl.ds(base + b * hr_rows, hr_rows)] = jnp.concatenate(
-                    [
-                        kvbuf[slot, s, b * hr_rows : (b + 1) * hr_rows, HD:LANES],
-                        kvbuf[slot, s, rows : rows + hr_rows, 64 * b : 64 * (b + 1)],
-                        ones,
-                    ],
-                    axis=1,
-                )
-
-    def tile(slot, t, first):
-        at = pl.ds(pl.multiple_of(t * rows, rows), rows)
-        kk = kvbuf[slot, :, 0:rows, :].reshape(keys, LANES)
+    tall = rows + hr_rows
+
+    quarter = half // 2
+
+    def unpack(slots, first_place):
+        ones = jnp.ones((hr_rows, LANES - HD), BF16)
+        for n, slot in enumerate(slots):
+            for m in range(quarter):
+                for b in range(2):
+                    base = (n * quarter + m) * rows + b * hr_rows
+                    vfull[base : base + hr_rows] = jnp.concatenate(
+                        [
+                            kvbuf[slot, first_place + m, b * hr_rows : (b + 1) * hr_rows, HD:LANES],
+                            kvbuf[slot, first_place + m, rows:tall, 64 * b : 64 * (b + 1)],
+                            ones,
+                        ],
+                        axis=1,
+                    )
+
+    wide = 2 * rows
+
+    def tile(slots, place, base, first):
+        at = pl.ds(pl.multiple_of(base, wide), wide)
+        kk = jnp.concatenate(
+            [
+                kvbuf[slot, place : place + quarter, 0:rows, :].reshape(quarter * rows, LANES)
+                for slot in slots
+            ],
+            axis=0,
+        )
         s = lax.dot_general(
             qfull[at], kk, (((1,), (1,)), ((), ())), preferred_element_type=F32
         )
@@ -255,61 +297,63 @@
             mix = mix + acc[at] * jnp.exp2(old - new)
         return at, mix, new
 
-    def attend(slot, first):
-        unpack(slot)
-
-        @pl.loop(0, ny)
-        def _(t):
-            at, mix, new = tile(slot, t, first)
+    def attend(slots, place, first):
+        unpack(slots, place)
+        for t in range(half):
+            at, mix, new = tile(slots, place, t * wide, first)
             acc[at] = mix
-            top[at] = jnp.broadcast_to(new, (rows, LANES))
-
-    attend(x, True)
-    for s in range(half):
-        wait_for(kvbuf.at[x_left, s], kv_r.at[x_left, s])
-        if s < half // 2:
-            send(kvbuf.at[x_left, s], kvbuf.at[x_left, s], xf_s.at[s], kv_r.at[x_left, s], right)
-    for s in range(half // 2, half):
-        wait_for(kvbuf.at[x_right, s], kv_r.at[x_right, s])
-        send(kvbuf.at[x_right, s], kvbuf.at[x_right, s], xf_s.at[s], kv_r.at[x_right, s], left)
-    attend(x_left, False)
-    for s in range(half // 2):
-        wait_for(kvbuf.at[x_right, s], kv_r.at[x_right, s])
-    attend(x_right, False)
-    for s in range(half):
-        wait_for(kvbuf.at[x_far, s], kv_r.at[x_far, s])
-    unpack(x_far)
-    lane = lax.broadcasted_iota(jnp.int32, (rows, LANES), 1)
-
-    @pl.loop(0, half)
-    def _(k):
-        at, mix, new = tile(x_far, (1 - core) * half + k, False)
-        acc[at] = jnp.where(lane >= LANES - 16, jnp.broadcast_to(new, (rows, LANES)), mix)
-        send(acc.at[at], accr.at[k], a_s.at[k], a_r.at[k], sibling)
-
-    @pl.loop(0, half)
-    def _(k):
-        at, mix, new = tile(x_far, core * half + k, False)
-        wait_for(accr.at[k], a_r.at[k])
-        other = accr[k]
-        other_top = other[:, LANES - 1 : LANES]
-        both = jnp.maximum(new, other_top)
-        total = mix * jnp.exp2(new - both) + other * jnp.exp2(other_top - both)
-        out = (total / total[:, HD : HD + 1]).astype(BF16)
-        for cc in range(2):
-            for zz in range(2):
-                src = (zz * 2 + cc) * block
-                ctxs[k, cc, zz * block : (zz + 1) * block] = out[src : src + block]
-        yd = core * half + k
-        for cc in range(2):
-            send_or_keep(
-                jnp.logical_and(yd == y, core == cc),
-                ctxs.at[k, cc],
-                cbuf.at[y],
-                c_s.at[k, cc],
-                c_r.at[y],
-                dev(yd, x, zh * 2 + cc),
-            )
+            top[at] = jnp.broadcast_to(new, (wide, LANES))
+
+    arrive(x_left, 1)
+    attend((x, x_left), 0, True)
+    spread(2)
+    arrive(x_right, 0)
+    arrive(x_far, 0)
+    arrive(x_far, 1)
+    attend((x_right, x_far), 0, False)
+    spread(3)
+    pass_on(2)
+    pass_on(3)
+    arrive(x_left, 3)
+    attend((x, x_left), 2, False)
+    arrive(x_right, 2)
+    arrive(x_far, 2)
+    arrive(x_far, 3)
+    last = (x_right, x_far)
+    unpack(last, 2)
+    lane = lax.broadcasted_iota(jnp.int32, (wide, LANES), 1)
+    for t in range(half // 2):
+        at, mix, new = tile(last, 2, (1 - core) * half * rows + t * wide, False)
+        acc[at] = jnp.where(lane >= LANES - 16, jnp.broadcast_to(new, (wide, LANES)), mix)
+        send(acc.at[at], accr.at[pl.ds(t * wide, wide)], a_s.at[t], a_r.at[t], sibling)
+    for t in range(half // 2):
+        at, mix, new = tile(last, 2, core * half * rows + t * wide, False)
+        acc[at] = mix
+        top[at] = jnp.broadcast_to(new, (wide, LANES))
+    for t in range(half // 2):
+        wait_for(accr.at[pl.ds(t * wide, wide)], a_r.at[t])
+        for k in range(2 * t, 2 * t + 2):
+            yd = core * half + k
+            at = pl.ds(pl.multiple_of(yd * rows, rows), rows)
+            other = accr[k * rows : (k + 1) * rows]
+            other_top = other[:, LANES - 1 : LANES]
+            new = top[at][:, 0:1]
+            both = jnp.maximum(new, other_top)
+            total = acc[at] * jnp.exp2(new - both) + other * jnp.exp2(other_top - both)
+            out = (total / total[:, HD : HD + 1]).astype(BF16)
+            for cc in range(2):
+                for zz in range(2):
+                    src = (zz * 2 + cc) * block
+                    ctxs[k, cc, zz * block : (zz + 1) * block] = out[src : src + block]
+            for cc in range(2):
+                send_or_keep(
+                    jnp.logical_and(yd == y, core == cc),
+                    ctxs.at[k, cc],
+                    cbuf.at[y],
+                    c_s.at[k, cc],
+                    c_r.at[y],
+                    dev(yd, x, zh * 2 + cc),
+                )
 
     own_w.wait()
     own_x.wait()
@@ -364,7 +408,6 @@
         def _():
             send(hs.at[zz], hr.at[1 - zz], h_s.at[zz], h_r.at[1 - zz], (dp, target, tp))
 
-    own_g.wait()
     for i in range(pieces):
         wait_for(
             nbuf.at[zh * 2 + 1 - core, pl.ds(i * step, step)], n_r.at[zh * 2 + 1 - core, i]
@@ -400,22 +443,6 @@
         def _():
             gpad[place] = jnp.zeros((rim, width), F32)
 
-    offset = rim - (KERNEL - 1) // 2
-    tall = 2 * rim
-    taps = taps_ref[...]
-    scale = scale_ref[...].reshape(1, -1)
-    shift = shift_ref[...].reshape(1, -1)
-
-    @pl.loop(0, rows // rim)
-    def _(r):
-        at = pl.multiple_of(r * rim, rim)
-        window = gpad[pl.ds(at, rim + tall)]
-        total = window[offset : offset + rim] * taps[0:1]
-        for k in range(1, KERNEL):
-            total = total + window[offset + k : offset + k + rim] * taps[k : k + 1]
-        u = total * scale + shift
-        conv_ref[pl.ds(at, rim)] = (u * jax.nn.sigmoid(u)).astype(BF16)
-
     for j in range(half):
         here = jnp.logical_and(core * half + j == y, core == parity)
 
@@ -428,7 +455,6 @@
         wait_for(kvbuf.at[x, j], xr_s.at[j])
         wait_for(kvbuf.at[x, j], xl_s.at[j])
         wait_for(kvbuf.at[x, j], xf_s.at[j])
-        wait_for(accr.at[j], a_s.at[j])
         for cc in range(2):
 
             @pl.when(jnp.logical_not(jnp.logical_and(core * half + j == y, core == cc)))
@@ -436,6 +462,8 @@
                 wait_for(ctxs.at[j, cc], c_s.at[j, cc])
 
     wait_for(wall.at[core], w_s)
+    for t in range(half // 2):
+        wait_for(accr.at[pl.ds(t * wide, wide)], a_s.at[t])
     for i in range(pieces):
         piece = pl.ds(i * step, step)
         wait_for(zs.at[piece], z_s.at[i])
@@ -448,6 +476,26 @@
         @pl.when(jnp.logical_and(target >= 0, target < n_ctx))
         def _():
             wait_for(hs.at[side], h_s.at[side])
+
+
+def convolve(att_in, gpad, taps_ref, scale_ref, shift_ref, att_ref, conv_ref):
+    rows = conv_ref.shape[0]
+    rim = (gpad.shape[0] - rows) // 2
+    att_ref[...] = att_in[...]
+    offset = rim - (KERNEL - 1) // 2
+    taps = taps_ref[...]
+    scale = scale_ref[...].reshape(1, -1)
+    shift = shift_ref[...].reshape(1, -1)
+
+    @pl.loop(0, rows // rim)
+    def _(r):
+        at = pl.multiple_of(r * rim, rim)
+        window = gpad[pl.ds(at, 3 * rim)]
+        total = window[offset : offset + rim] * taps[0:1]
+        for k in range(1, KERNEL):
+            total = total + window[offset + k : offset + k + rim] * taps[k : k + 1]
+        u = total * scale + shift
+        conv_ref[pl.ds(at, rim)] = (u * jax.nn.sigmoid(u)).astype(BF16)
 
 
 def shards(
@@ -485,18 +533,18 @@
         pltpu.VMEM((half * rows, LANES), BF16),
         pltpu.VMEM((ny * rows, LANES), F32),
         pltpu.VMEM((ny * rows, LANES), F32),
-        pltpu.VMEM((half, rows, LANES), F32),
+        pltpu.VMEM((half * rows, LANES), F32),
         pltpu.VMEM((half, 2, 2 * block, LANES), BF16),
         pltpu.VMEM((ny, 2 * block, LANES), BF16),
         pltpu.VMEM((2 * block, ny * HD), BF16),
         pltpu.VMEM((2, half * HD, model), BF16),
+        pltpu.VMEM((model, 2, columns), BF16),
         pltpu.VMEM((model, 2 * columns), BF16),
         pltpu.VMEM((block, model), BF16),
         pltpu.VMEM((block, model), F32),
         pltpu.VMEM((block, model), BF16),
         pltpu.VMEM((block, model), BF16),
         pltpu.VMEM((4, block, model), BF16),
-        pltpu.VMEM((rows + 2 * rim, columns), F32),
         pltpu.VMEM((2, rim, columns), BF16),
         pltpu.VMEM((2, rim, columns), BF16),
         dma((half,)),
@@ -523,13 +571,13 @@
         dma((2,)),
         dma((2,)),
     ]
-    return pl.pallas_call(
+    attended, padded = pl.pallas_call(
         functools.partial(kernel, ny, nx),
         out_shape=(
             jax.ShapeDtypeStruct((block, model), BF16),
-            jax.ShapeDtypeStruct((rows, columns), BF16),
+            jax.ShapeDtypeStruct((rows + 2 * rim, columns), F32),
         ),
-        in_specs=[anywhere, vmem, vmem, vmem, anywhere, vmem, vmem, anywhere, vmem, vmem, vmem],
+        in_specs=[anywhere, vmem, vmem, vmem, anywhere, vmem, vmem, anywhere],
         out_specs=(vmem, vmem),
         scratch_shapes=scratch,
         compiler_params=pltpu.CompilerParams(
@@ -546,11 +594,17 @@
         out_weight,
         norm_gain,
         norm_bias,
-        glu_weight.reshape(glu_weight.shape[0], 2 * columns),
-        conv_weight,
-        conv_scale,
-        conv_shift,
+        glu_weight,
     )
+    return pl.pallas_call(
+        convolve,
+        out_shape=(
+            jax.ShapeDtypeStruct((block, model), BF16),
+            jax.ShapeDtypeStruct((rows, columns), BF16),
+        ),
+        in_specs=[vmem] * 5,
+        out_specs=(vmem, vmem),
+    )(attended, padded, conv_weight, conv_scale, conv_shift)
 
 
 def solution(mesh):

time: 87.7 us -> 81.2 us (0.926)
  local copies, waits for them, and re-layouts: 6.71 us -> 0 us
    unnamed x3 -> x0, local copies, waits for them, and re-layouts: 6.71 us -> none
    pallas_call x0 -> x1, Pallas kernels: none -> 3.89 us  [shards(): pl.pallas_call(convolve, out_shape=(jax.ShapeDtypeStruct((block, model),...]
    pallas_call x1, Pallas kernels: 80 us -> 76.5 us  [shards(): pl.pallas_call(functools.partial(kernel, ny, nx), out_shape=(jax.ShapeDty...]
where the time goes in v2:
time: 81.2 us; the launch traced here: 81 us
  Pallas kernels  80.4 us (99%)
    pallas_call x1, Pallas kernels, shards(): pl.pallas_call(functools.partial(kernel, ny, nx), out_shape=(jax.ShapeDty...  76.5 us
    pallas_call x1, Pallas kernels, shards(): pl.pallas_call(convolve, out_shape=(jax.ShapeDtypeStruct((block, model),...  3.89 us

profile of v2, /device:TPU:137, one launch (start us, length us, event | category | flops | bytes accessed | tf_op | source)
XLA Modules:
  0.0 81.0 jit_solution(9221610426461088468)
XLA Ops:
  0.6 76.5 %shard_map.122 = (bf16[48,1536]{1,0:T(8,128)(2,1)}, f32[224,384]{1,0:T(8,128)}) custom-call(bf16[192,1536]{1,0:T(8,128)(2,1)} %resid_ref.1, bf16[192,384]{1,0:T(8,128)(2,1)} %q_ref.1, bf16[192,384]{1,0:T(8,128)(2,1)} %k_ref.1, bf16[192,384]{1,0:T(8,128)(2,1)} %v_ref.1, bf16[384,1536]{1,0:T(8,128)(2,1)} %w_ref.1, f32[1536]{0:T(1024)} %gain_ref.1, ...), custom_call_target="tpu_custom_call" | custom-call | flops 3000000000 | bytes 10000000 | tf_op jit(solution)/shard_map/pallas_call | solution.py:574
  77.2 3.9 %shard_map.123 = (bf16[48,1536]{1,0:T(8,128)(2,1)}, bf16[192,384]{1,0:T(8,128)(2,1)}) custom-call(bf16[48,1536]{1,0:T(8,128)(2,1)} %get-tuple-element.4.att_in, f32[224,384]{1,0:T(8,128)} %get-tuple-element.5.gpad, f32[31,384]{1,0:T(8,128)} %taps_ref.1, f32[384]{0:T(512)} %scale_ref.1, f32[384]{0:T(512)} %shift_ref.1), custom_call_target="tpu_custom_call" | custom-call | tf_op jit(solution)/shard_map/pallas_call | solution.py:599

commit v3 on v2

--- a/solution.py
+++ b/solution.py
@@ -44,16 +44,21 @@
 def kernel(
     ny,
     nx,
-    resid_ref,
+    resid_in,
+    q_in,
+    k_in,
+    v_in,
+    w_ref,
+    gain_in,
+    bias_in,
+    glu_ref,
+    att_ref,
+    gpad,
     q_ref,
     k_ref,
     v_ref,
-    w_ref,
     gain_ref,
     bias_ref,
-    glu_ref,
-    att_ref,
-    gpad,
     qs,
     kvs,
     qbuf,
@@ -101,7 +106,7 @@
     h_r,
 ):
     half = ny // 2
-    rows = q_ref.shape[0]
+    rows = q_in.shape[0]
     block = rows // 4
     rim = gpad.shape[0] - rows
     rim = rim // 2
@@ -122,6 +127,24 @@
     x_right, x_left, x_far = (x + 1) % nx, (x + nx - 1) % nx, (x + 2) % nx
     right, left = dev(y, x_right, tp), dev(y, x_left, tp)
 
+    loads = [
+        pltpu.make_async_copy(src, dst, l_r.at[i])
+        for i, (src, dst) in enumerate(
+            (
+                (k_in, k_ref),
+                (v_in, v_ref),
+                (q_in, q_ref),
+                (w_ref, wall.at[core]),
+                (glu_ref, graw),
+                (resid_in.at[pl.ds(pl.multiple_of(tp * block, block), block)], resid),
+                (gain_in, gain_ref),
+                (bias_in, bias_ref),
+            )
+        )
+    ]
+    load_k, load_v, load_q, own_w, own_g, own_x, load_gain, load_bias = loads
+    for load in loads:
+        load.start()
     barrier = pltpu.get_barrier_semaphore()
 
     def greet(device):
@@ -137,17 +160,10 @@
     greet((dp, (ctx + 1) % n_ctx, tp))
     greet((dp, (ctx + n_ctx - 1) % n_ctx, tp))
 
-    own_w = pltpu.make_async_copy(w_ref, wall.at[core], l_r.at[0])
-    own_w.start()
-    own_g = pltpu.make_async_copy(glu_ref, graw, l_r.at[1])
-    own_g.start()
-    own_x = pltpu.make_async_copy(
-        resid_ref.at[pl.ds(pl.multiple_of(tp * block, block), block)], resid, l_r.at[2]
-    )
-    own_x.start()
-
     cut = rows * 3 // 4
     part = rows - cut
+    load_k.wait()
+    load_v.wait()
     for j in range(half):
         lo = HD * j
         kvs[j, 0:rows] = jnp.concatenate(
@@ -157,6 +173,41 @@
             [v_ref[0 : rows // 2, lo + 32 : lo + HD], v_ref[rows // 2 : rows, lo + 32 : lo + HD]],
             axis=1,
         )
+
+    pl.semaphore_wait(barrier, 2 * (ny - 1) + 6)
+
+    def rank(distance):
+        sign = distance // (half + 1)
+        fold = distance + sign * (ny - 2 * distance)
+        odd = distance % 2
+        return odd * (fold // 2 * 2 + sign) + (1 - odd) * (fold // 2 + fold // half + sign)
+
+    near = [0]
+    for o in range(1, half):
+        near += [o, ny - o]
+    near.append(half)
+
+    def to_head(o, src, dst, send_sem, recv_sem):
+        head = (y + o) % ny
+        j = head % half
+        device = dev(head, x, zh * 2 + parity)
+
+        @pl.when(head // half == core)
+        def _():
+            if o == 0:
+                send_or_keep(core == parity, src.at[j], dst, send_sem.at[j], recv_sem, device)
+            else:
+                send(src.at[j], dst, send_sem.at[j], recv_sem, device)
+
+    def kv_to_head(o):
+        place = rank((ny - o) % ny)
+        to_head(o, kvs, kvbuf.at[x, place], skv_s, kv_r.at[x, place])
+
+    for o in near[:3]:
+        kv_to_head(o)
+    load_q.wait()
+    for j in range(half):
+        lo = HD * j
         qs[j] = jnp.concatenate(
             [
                 q_ref[0:cut, lo : lo + HD],
@@ -166,45 +217,10 @@
             ],
             axis=1,
         )
-
-    pl.semaphore_wait(barrier, 2 * (ny - 1) + 6)
-
-    def rank(distance):
-        sign = distance // (half + 1)
-        fold = distance + sign * (ny - 2 * distance)
-        odd = distance % 2
-        return odd * (fold // 2 * 2 + sign) + (1 - odd) * (fold // 2 + fold // half + sign)
-
-    near = [0]
-    for o in range(1, half):
-        near += [o, ny - o]
-    near.append(half)
-
-    def to_head(o, src, dst, send_sem, recv_sem):
-        head = (y + o) % ny
-        j = head % half
-        device = dev(head, x, zh * 2 + parity)
-
-        @pl.when(head // half == core)
-        def _():
-            if o == 0:
-                send_or_keep(core == parity, src.at[j], dst, send_sem.at[j], recv_sem, device)
-            else:
-                send(src.at[j], dst, send_sem.at[j], recv_sem, device)
-
     for o in near[::-1]:
         to_head(o, qs, qbuf.at[y], sq_s, q_r.at[y])
-    for o in near:
-        place = rank((ny - o) % ny)
-        to_head(o, kvs, kvbuf.at[x, place], skv_s, kv_r.at[x, place])
-
-    for i in range(half):
-        ys = 2 * ((y // 2 + i + 1) % half) + core
-        wait_for(qbuf.at[ys], q_r.at[ys])
-        send(qbuf.at[ys], qbuf.at[ys], qf_s.at[i], q_r.at[ys], sibling)
-    send(w_ref, wall.at[core], w_s, w_r, sibling)
-    own_g.wait()
-    span = graw.shape[0] // half
+    for o in near[3:]:
+        kv_to_head(o)
 
     def spread(s):
         wait_for(kvbuf.at[x, s], kv_r.at[x, s])
@@ -218,6 +234,8 @@
 
     def arrive(slot, s):
         wait_for(kvbuf.at[slot, s], kv_r.at[slot, s])
+
+    span = graw.shape[0] // half
 
     def relayout(i):
         @pl.loop(0, span // 16)
@@ -227,13 +245,16 @@
             gw[at] = jnp.concatenate([pair[:, 0, :], pair[:, 1, :]], axis=1).astype(BF16)
 
     spread(0)
+    for i in range(half):
+        ys = 2 * ((y // 2 + i + 1) % half) + core
+        wait_for(qbuf.at[ys], q_r.at[ys])
+        send(qbuf.at[ys], qbuf.at[ys], qf_s.at[i], q_r.at[ys], sibling)
+    own_g.wait()
     relayout(0)
     spread(1)
+    send(w_ref, wall.at[core], w_s, w_r, sibling)
     relayout(1)
-    relayout(2)
     pass_on(0)
-    relayout(3)
-    pass_on(1)
     for i in range(half):
         ys = 2 * ((y // 2 + i) % half) + 1 - core
         wait_for(qbuf.at[ys], q_r.at[ys])
@@ -250,6 +271,8 @@
             axis=1,
         )
 
+    pass_on(1)
+    relayout(2)
     factor = math.log2(math.e) / math.sqrt(HD)
     hr_rows = rows // 2
     tall = rows + hr_rows
@@ -307,11 +330,12 @@
     arrive(x_left, 1)
     attend((x, x_left), 0, True)
     spread(2)
+    relayout(3)
+    spread(3)
     arrive(x_right, 0)
     arrive(x_far, 0)
     arrive(x_far, 1)
     attend((x_right, x_far), 0, False)
-    spread(3)
     pass_on(2)
     pass_on(3)
     arrive(x_left, 3)
@@ -355,8 +379,8 @@
                     dev(yd, x, zh * 2 + cc),
                 )
 
-    own_w.wait()
-    own_x.wait()
+    for load in (own_w, own_x, load_gain, load_bias):
+        load.wait()
     wait_for(wall.at[1 - core], w_r)
     for h in range(ny):
         wait_for(cbuf.at[h], c_r.at[h])
@@ -487,15 +511,20 @@
     scale = scale_ref[...].reshape(1, -1)
     shift = shift_ref[...].reshape(1, -1)
 
-    @pl.loop(0, rows // rim)
-    def _(r):
-        at = pl.multiple_of(r * rim, rim)
-        window = gpad[pl.ds(at, 3 * rim)]
-        total = window[offset : offset + rim] * taps[0:1]
-        for k in range(1, KERNEL):
-            total = total + window[offset + k : offset + k + rim] * taps[k : k + 1]
-        u = total * scale + shift
-        conv_ref[pl.ds(at, rim)] = (u * jax.nn.sigmoid(u)).astype(BF16)
+    for r in range(0, rows, 4 * rim):
+        for lane in range(0, conv_ref.shape[1], LANES):
+            at = slice(lane, lane + LANES)
+            window = gpad[r : r + 6 * rim, at]
+            total = None
+            for turn in range(8):
+                places = [p for p in range(offset, offset + KERNEL) if p % 8 == turn]
+                top = places[-1] + 4 * rim
+                turned = window[turn : turn + (top - turn) // 8 * 8]
+                for p in places:
+                    term = turned[p - turn : p - turn + 4 * rim] * taps[p - offset : p - offset + 1, at]
+                    total = term if total is None else total + term
+            u = total * scale[:, at] + shift[:, at]
+            conv_ref[r : r + 4 * rim, at] = (u * jax.nn.sigmoid(u)).astype(BF16)
 
 
 def shards(
@@ -525,6 +554,11 @@
     dma = pltpu.SemaphoreType.DMA
     tall = rows + rows // 2
     scratch = [
+        pltpu.VMEM((rows, columns), BF16),
+        pltpu.VMEM((rows, columns), BF16),
+        pltpu.VMEM((rows, columns), BF16),
+        pltpu.VMEM((model,), F32),
+        pltpu.VMEM((model,), F32),
         pltpu.VMEM((half, rows * 3 // 4, LANES), BF16),
         pltpu.VMEM((half, tall, LANES), BF16),
         pltpu.VMEM((ny, rows * 3 // 4, LANES), BF16),
@@ -561,7 +595,7 @@
         dma((ny,)),
         dma,
         dma,
-        dma((3,)),
+        dma((8,)),
         dma((pieces,)),
         dma((pieces,)),
         dma((pieces,)),
@@ -577,7 +611,7 @@
             jax.ShapeDtypeStruct((block, model), BF16),
             jax.ShapeDtypeStruct((rows + 2 * rim, columns), F32),
         ),
-        in_specs=[anywhere, vmem, vmem, vmem, anywhere, vmem, vmem, anywhere],
+        in_specs=[anywhere] * 8,
         out_specs=(vmem, vmem),
         scratch_shapes=scratch,
         compiler_params=pltpu.CompilerParams(

time: 81.2 us -> 76.9 us (0.947)
  Pallas kernels: 80.4 us -> 76.2 us
    pallas_call x1, Pallas kernels: 76.5 us -> 73 us  [shards(): pl.pallas_call(functools.partial(kernel, ny, nx), out_shape=(jax.ShapeDty...]
where the time goes in v3:
time: 76.9 us; the launch traced here: 76.8 us
  Pallas kernels  76.2 us (99%)
    pallas_call x1, Pallas kernels, shards(): pl.pallas_call(functools.partial(kernel, ny, nx), out_shape=(jax.ShapeDty...  73 us
    pallas_call x1, Pallas kernels, shards(): pl.pallas_call(convolve, out_shape=(jax.ShapeDtypeStruct((block, model),...  3.21 us

profile of v3, /device:TPU:137, one launch (start us, length us, event | category | flops | bytes accessed | tf_op | source)
XLA Modules:
  0.0 76.8 jit_solution(14698636154488498011)
XLA Ops:
  0.6 73.0 %shard_map.122 = (bf16[48,1536]{1,0:T(8,128)(2,1)}, f32[224,384]{1,0:T(8,128)}) custom-call(bf16[192,1536]{1,0:T(8,128)(2,1)} %resid_in.1, bf16[192,384]{1,0:T(8,128)(2,1)} %q_in.1, bf16[192,384]{1,0:T(8,128)(2,1)} %k_in.1, bf16[192,384]{1,0:T(8,128)(2,1)} %v_in.1, bf16[384,1536]{1,0:T(8,128)(2,1)} %w_ref.1, f32[1536]{0:T(1024)} %gain_in.1, f32[1536]{0:T(1024)} %bias_in.1, ...), custom_call_target="tpu_custom_call" | custom-call | flops 3000000000 | bytes 10000000 | tf_op jit(solution)/shard_map/pallas_call | solution.py:608
  73.6 3.2 %shard_map.123 = (bf16[48,1536]{1,0:T(8,128)(2,1)}, bf16[192,384]{1,0:T(8,128)(2,1)}) custom-call(bf16[48,1536]{1,0:T(8,128)(2,1)} %get-tuple-element.4.att_in, f32[224,384]{1,0:T(8,128)} %get-tuple-element.5.gpad, f32[31,384]{1,0:T(8,128)} %taps_ref.1, f32[384]{0:T(512)} %scale_ref.1, f32[384]{0:T(512)} %shift_ref.1), custom_call_target="tpu_custom_call" | custom-call | tf_op jit(solution)/shard_map/pallas_call | solution.py:633

commit v4 on v3

--- a/solution.py
+++ b/solution.py
@@ -75,9 +75,6 @@
     graw,
     gw,
     resid,
-    own,
-    zs,
-    zr,
     nbuf,
     hs,
     hr,
@@ -98,10 +95,14 @@
     l_r,
     z_s,
     z_r,
-    nz_s,
-    ns_s,
-    nf_s,
+    n_s,
     n_r,
+    wa_s,
+    wa_r,
+    wb_s,
+    wb_r,
+    wf_s,
+    wf_r,
     h_s,
     h_r,
 ):
@@ -123,7 +124,13 @@
         return (dp, yy * nx + xx, tt)
 
     sibling = (dp, ctx, zh * 2 + 1 - core)
-    partner = (dp, ctx, (1 - zh) * 2 + core)
+    away, away_sibling = (1 - zh) * 2 + core, (1 - zh) * 2 + 1 - core
+    partner = (dp, ctx, away)
+    n_dp = lax.axis_size("dp")
+    above = (zh * n_dp + dp + 1) % (2 * n_dp)
+    below = (zh * n_dp + dp + 2 * n_dp - 1) % (2 * n_dp)
+    up = (above % n_dp, ctx, above // n_dp * 2 + core)
+    down = (below % n_dp, ctx, below // n_dp * 2 + core)
     x_right, x_left, x_far = (x + 1) % nx, (x + nx - 1) % nx, (x + 2) % nx
     right, left = dev(y, x_right, tp), dev(y, x_left, tp)
 
@@ -134,15 +141,19 @@
                 (k_in, k_ref),
                 (v_in, v_ref),
                 (q_in, q_ref),
-                (w_ref, wall.at[core]),
+                (w_ref, wall.at[tp]),
                 (glu_ref, graw),
-                (resid_in.at[pl.ds(pl.multiple_of(tp * block, block), block)], resid),
+                (resid_in.at[pl.ds(pl.multiple_of(core * block, block), block)], resid.at[0:block]),
+                (
+                    resid_in.at[pl.ds(pl.multiple_of((2 + core) * block, block), block)],
+                    resid.at[block : 2 * block],
+                ),
                 (gain_in, gain_ref),
                 (bias_in, bias_ref),
             )
         )
     ]
-    load_k, load_v, load_q, own_w, own_g, own_x, load_gain, load_bias = loads
+    load_k, load_v, load_q, own_w, own_g, own_x, own_x2, load_gain, load_bias = loads
     for load in loads:
         load.start()
     barrier = pltpu.get_barrier_semaphore()
@@ -155,6 +166,8 @@
             greet(dev((y + o) % ny, x, zh * 2 + cc))
     greet(sibling)
     greet(partner)
+    greet(up)
+    greet(down)
     greet(right)
     greet(left)
     greet((dp, (ctx + 1) % n_ctx, tp))
@@ -174,7 +187,7 @@
             axis=1,
         )
 
-    pl.semaphore_wait(barrier, 2 * (ny - 1) + 6)
+    pl.semaphore_wait(barrier, 2 * (ny - 1) + 8)
 
     def rank(distance):
         sign = distance // (half + 1)
@@ -205,6 +218,43 @@
 
     for o in near[:3]:
         kv_to_head(o)
+    pieces = wa_s.shape[0]
+    piece_rows = w_ref.shape[0] // (2 * pieces)
+
+    def piece_of(ref, side, i):
+        start = side * (w_ref.shape[0] // 2) + i * piece_rows
+        return ref.at[pl.ds(pl.multiple_of(start, 16), piece_rows)]
+
+    @pl.when(dp == 0)
+    def _():
+        for i in range(pieces):
+            src, dst = piece_of(w_ref, 0, i), piece_of(wall.at[tp], 0, i)
+            send(src, dst, wa_s.at[i], wa_r.at[i], down)
+
+    @pl.when(dp == n_dp - 1)
+    def _():
+        for i in range(pieces):
+            src, dst = piece_of(w_ref, 1, i), piece_of(wall.at[tp], 1, i)
+            send(src, dst, wb_s.at[i], wb_r.at[i], up)
+
+    def relay(slot):
+        for side, hop, s_sem, r_sem, target in (
+            (0, n_dp - 1 - dp, wa_s, wa_r, down),
+            (1, dp, wb_s, wb_r, up),
+        ):
+            i = slot - hop
+
+            @pl.when(jnp.logical_and(i >= 0, i < pieces))
+            def _():
+                held = piece_of(wall.at[away], side, i)
+                wait_for(held, r_sem.at[i])
+
+                @pl.when(hop < n_dp - 1)
+                def _():
+                    send(held, held, s_sem.at[i], r_sem.at[i], target)
+
+                send(held, held, wf_s.at[side, i], wf_r.at[side, i], sibling)
+
     load_q.wait()
     for j in range(half):
         lo = HD * j
@@ -249,10 +299,12 @@
         ys = 2 * ((y // 2 + i + 1) % half) + core
         wait_for(qbuf.at[ys], q_r.at[ys])
         send(qbuf.at[ys], qbuf.at[ys], qf_s.at[i], q_r.at[ys], sibling)
+    relay(0)
     own_g.wait()
     relayout(0)
     spread(1)
-    send(w_ref, wall.at[core], w_s, w_r, sibling)
+    send(w_ref, wall.at[tp], w_s, w_r, sibling)
+    relay(1)
     relayout(1)
     pass_on(0)
     for i in range(half):
@@ -272,6 +324,7 @@
         )
 
     pass_on(1)
+    relay(2)
     relayout(2)
     factor = math.log2(math.e) / math.sqrt(HD)
     hr_rows = rows // 2
@@ -329,17 +382,21 @@
 
     arrive(x_left, 1)
     attend((x, x_left), 0, True)
+    relay(3)
     spread(2)
     relayout(3)
     spread(3)
+    relay(4)
     arrive(x_right, 0)
     arrive(x_far, 0)
     arrive(x_far, 1)
     attend((x_right, x_far), 0, False)
     pass_on(2)
     pass_on(3)
+    relay(5)
     arrive(x_left, 3)
     attend((x, x_left), 2, False)
+    relay(6)
     arrive(x_right, 2)
     arrive(x_far, 2)
     arrive(x_far, 3)
@@ -350,6 +407,7 @@
         at, mix, new = tile(last, 2, (1 - core) * half * rows + t * wide, False)
         acc[at] = jnp.where(lane >= LANES - 16, jnp.broadcast_to(new, (wide, LANES)), mix)
         send(acc.at[at], accr.at[pl.ds(t * wide, wide)], a_s.at[t], a_r.at[t], sibling)
+    relay(7)
     for t in range(half // 2):
         at, mix, new = tile(last, 2, core * half * rows + t * wide, False)
         acc[at] = mix
@@ -379,79 +437,53 @@
                     dev(yd, x, zh * 2 + cc),
                 )
 
-    for load in (own_w, own_x, load_gain, load_bias):
+    for slot in range(n_dp + 4, n_dp + pieces - 1):
+        relay(slot)
+    for load in (own_w, own_x, own_x2, load_gain, load_bias):
         load.wait()
-    wait_for(wall.at[1 - core], w_r)
-    for h in range(ny):
-        wait_for(cbuf.at[h], c_r.at[h])
-        cat[:, HD * h : HD * (h + 1)] = cbuf[h, :, 0:HD]
-
-    def project(zz):
-        return jnp.dot(
-            cat[pl.ds(pl.multiple_of(zz * block, block), block)],
-            wall[...].reshape(wall.shape[0] * wall.shape[1], wall.shape[2]),
-            preferred_element_type=F32,
-        )
-
-    pieces = z_s.shape[0]
-    step = block // pieces
-    zs[...] = project(1 - zh).astype(BF16)
-    for i in range(pieces):
-        send(
-            zs.at[pl.ds(i * step, step)],
-            zr.at[pl.ds(i * step, step)],
-            z_s.at[i],
-            z_r.at[i],
-            partner,
-        )
-    own[...] = project(zh) + resid[...].astype(F32)
-    for i in range(pieces):
-        piece = pl.ds(i * step, step)
-        wait_for(zr.at[piece], z_r.at[i])
-        attended = (own[piece] + zr[piece].astype(F32)).astype(BF16)
-        att_ref[piece] = attended
-        full = attended.astype(F32)
-        centred = full - jnp.mean(full, axis=1, keepdims=True)
-        var = jnp.mean(centred * centred, axis=1, keepdims=True)
-        normed = centred * lax.rsqrt(var + 1e-05) * gain_ref[...].reshape(1, -1)
-        nbuf[tp, piece] = (normed + bias_ref[...].reshape(1, -1)).astype(BF16)
-        send(nbuf.at[tp, piece], nbuf.at[tp, piece], nz_s.at[i], n_r.at[tp, i], partner)
-        send(nbuf.at[tp, piece], nbuf.at[tp, piece], ns_s.at[i], n_r.at[tp, i], sibling)
-
-    def gate(zz):
-        data = nbuf[pl.ds(zz * 2, 2)].reshape(2 * block, nbuf.shape[2])
-        projected = jnp.dot(data, gw[...], preferred_element_type=F32)
+    wait_for(wall.at[zh * 2 + 1 - core], w_r)
+    total = resid[...].astype(F32)
+    for g in range(2):
+        for j in range(half):
+            wait_for(cbuf.at[g * half + j], c_r.at[g * half + j])
+            cat[zh, g, :, HD * j : HD * (j + 1)] = cbuf[g * half + j, :, 0:HD]
+        send(cat.at[zh, g], cat.at[zh, g], z_s.at[g], z_r.at[g], partner)
+    for g in range(2):
+        total += jnp.dot(cat[zh, g], wall[zh * 2 + g], preferred_element_type=F32)
+    for side in range(2):
+        for i in range(pieces):
+            wait_for(piece_of(wall.at[away_sibling], side, i), wf_r.at[side, i])
+    for g in range(2):
+        wait_for(cat.at[1 - zh, g], z_r.at[g])
+        total += jnp.dot(cat[1 - zh, g], wall[(1 - zh) * 2 + g], preferred_element_type=F32)
+    attended = total.astype(BF16)
+    resid[...] = attended
+    att_ref[...] = resid[pl.ds(pl.multiple_of(zh * block, block), block)]
+    full = attended.astype(F32)
+    centred = full - jnp.mean(full, axis=1, keepdims=True)
+    var = jnp.mean(centred * centred, axis=1, keepdims=True)
+    normed = centred * lax.rsqrt(var + 1e-05) * gain_ref[...].reshape(1, -1)
+    nbuf[core] = (normed + bias_ref[...].reshape(1, -1)).astype(BF16)
+    send(nbuf.at[core], nbuf.at[core], n_s, n_r, sibling)
+
+    def gate(cc):
+        projected = jnp.dot(nbuf[cc], gw[...], preferred_element_type=F32)
         gated = projected[:, 0:width] * jax.nn.sigmoid(projected[:, width:])
-        base = pl.multiple_of(rim + zz * 2 * block, 16)
-        gpad[pl.ds(base, 2 * block)] = gated.astype(BF16).astype(F32)
-        edge = pl.multiple_of(rim + zz * (rows - rim), 16)
-        hs[zz] = gpad[pl.ds(edge, rim)].astype(BF16)
-        target = ctx + 2 * zz - 1
+        gated = gated.astype(BF16).astype(F32)
+        for zz in range(2):
+            base = pl.multiple_of(rim + (zz * 2 + cc) * block, 16)
+            gpad[pl.ds(base, block)] = gated[zz * block : (zz + 1) * block]
+        edge = pl.multiple_of(rim + cc * (rows - rim), 16)
+        hs[cc] = gpad[pl.ds(edge, rim)].astype(BF16)
+        target = ctx + 2 * cc - 1
 
         @pl.when(jnp.logical_and(target >= 0, target < n_ctx))
         def _():
-            send(hs.at[zz], hr.at[1 - zz], h_s.at[zz], h_r.at[1 - zz], (dp, target, tp))
-
-    for i in range(pieces):
-        wait_for(
-            nbuf.at[zh * 2 + 1 - core, pl.ds(i * step, step)], n_r.at[zh * 2 + 1 - core, i]
-        )
-    gate(zh)
-    tp_other = (1 - zh) * 2 + core
-    for i in range(pieces):
-        piece = pl.ds(i * step, step)
-        wait_for(nbuf.at[tp_other, piece], n_r.at[tp_other, i])
-        send(
-            nbuf.at[tp_other, piece],
-            nbuf.at[tp_other, piece],
-            nf_s.at[i],
-            n_r.at[tp_other, i],
-            sibling,
-        )
-    for i in range(pieces):
-        tp_last = (1 - zh) * 2 + 1 - core
-        wait_for(nbuf.at[tp_last, pl.ds(i * step, step)], n_r.at[tp_last, i])
-    gate(1 - zh)
+            send(hs.at[cc], hr.at[1 - cc], h_s.at[cc], h_r.at[1 - cc], (dp, target, tp))
+
+    gate(core)
+    wait_for(nbuf.at[1 - core], n_r)
+    gate(1 - core)
 
     for side in range(2):
         source = ctx + 2 * side - 1
@@ -485,15 +517,17 @@
             def _():
                 wait_for(ctxs.at[j, cc], c_s.at[j, cc])
 
-    wait_for(wall.at[core], w_s)
+    wait_for(wall.at[tp], w_s)
     for t in range(half // 2):
         wait_for(accr.at[pl.ds(t * wide, wide)], a_s.at[t])
     for i in range(pieces):
-        piece = pl.ds(i * step, step)
-        wait_for(zs.at[piece], z_s.at[i])
-        wait_for(nbuf.at[tp, piece], nz_s.at[i])
-        wait_for(nbuf.at[tp, piece], ns_s.at[i])
-        wait_for(nbuf.at[tp_other, piece], nf_s.at[i])
+        wait_for(piece_of(w_ref, 0, i), wa_s.at[i])
+        wait_for(piece_of(w_ref, 1, i), wb_s.at[i])
+        for side in range(2):
+            wait_for(piece_of(w_ref, side, i), wf_s.at[side, i])
+    for g in range(2):
+        wait_for(cat.at[zh, g], z_s.at[g])
+    wait_for(nbuf.at[core], n_s)
     for side in range(2):
         target = ctx + 2 * side - 1
 
@@ -547,7 +581,7 @@
     nx = n_ctx // ny
     model = residual_in.shape[1]
     block = rows // 4
-    pieces = block // 16
+    pieces = columns // 64
     rim = 16
     vmem = pl.BlockSpec(memory_space=pltpu.VMEM)
     anywhere = pl.BlockSpec(memory_space=pl.ANY)
@@ -570,15 +604,12 @@
         pltpu.VMEM((half * rows, LANES), F32),
         pltpu.VMEM((half, 2, 2 * block, LANES), BF16),
         pltpu.VMEM((ny, 2 * block, LANES), BF16),
-        pltpu.VMEM((2 * block, ny * HD), BF16),
-        pltpu.VMEM((2, half * HD, model), BF16),
+        pltpu.VMEM((2, 2, 2 * block, columns), BF16),
+        pltpu.VMEM((4, columns, model), BF16),
         pltpu.VMEM((model, 2, columns), BF16),
         pltpu.VMEM((model, 2 * columns), BF16),
-        pltpu.VMEM((block, model), BF16),
-        pltpu.VMEM((block, model), F32),
-        pltpu.VMEM((block, model), BF16),
-        pltpu.VMEM((block, model), BF16),
-        pltpu.VMEM((4, block, model), BF16),
+        pltpu.VMEM((2 * block, model), BF16),
+        pltpu.VMEM((2, 2 * block, model), BF16),
         pltpu.VMEM((2, rim, columns), BF16),
         pltpu.VMEM((2, rim, columns), BF16),
         dma((half,)),
@@ -595,13 +626,17 @@
         dma((ny,)),
         dma,
         dma,
-        dma((8,)),
+        dma((9,)),
+        dma((2,)),
+        dma((2,)),
+        dma,
+        dma,
         dma((pieces,)),
         dma((pieces,)),
         dma((pieces,)),
         dma((pieces,)),
-        dma((pieces,)),
-        dma((4, pieces)),
+        dma((2, pieces)),
+        dma((2, pieces)),
         dma((2,)),
         dma((2,)),
     ]

time: 76.9 us -> 77.4 us (level)
  the two profiles are of different devices: /device:TPU:137 before, /device:TPU:23 now
where the time goes in v4:
time: 77.4 us; the launch traced here: 77.2 us
  Pallas kernels  76.6 us (99%)
    pallas_call x1, Pallas kernels, shards(): pl.pallas_call(functools.partial(kernel, ny, nx), out_shape=(jax.ShapeDty...  73.4 us
    pallas_call x1, Pallas kernels, shards(): pl.pallas_call(convolve, out_shape=(jax.ShapeDtypeStruct((block, model),...  3.21 us

profile of v4, /device:TPU:23, one launch (start us, length us, event | category | flops | bytes accessed | tf_op | source)
XLA Modules:
  0.0 77.2 jit_solution(16248889940281335169)
XLA Ops:
  0.6 73.4 %shard_map.122 = (bf16[48,1536]{1,0:T(8,128)(2,1)}, f32[224,384]{1,0:T(8,128)}) custom-call(bf16[192,1536]{1,0:T(8,128)(2,1)} %resid_in.1, bf16[192,384]{1,0:T(8,128)(2,1)} %q_in.1, bf16[192,384]{1,0:T(8,128)(2,1)} %k_in.1, bf16[192,384]{1,0:T(8,128)(2,1)} %v_in.1, bf16[384,1536]{1,0:T(8,128)(2,1)} %w_ref.1, f32[1536]{0:T(1024)} %gain_in.1, f32[1536]{0:T(1024)} %bias_in.1, ...), custom_call_target="tpu_custom_call" | custom-call | flops 3000000000 | bytes 10000000 | tf_op jit(solution)/shard_map/pallas_call | solution.py:643
  74.0 3.2 %shard_map.123 = (bf16[48,1536]{1,0:T(8,128)(2,1)}, bf16[192,384]{1,0:T(8,128)(2,1)}) custom-call(bf16[48,1536]{1,0:T(8,128)(2,1)} %get-tuple-element.4.att_in, f32[224,384]{1,0:T(8,128)} %get-tuple-element.5.gpad, f32[31,384]{1,0:T(8,128)} %taps_ref.1, f32[384]{0:T(512)} %scale_ref.1, f32[384]{0:T(512)} %shift_ref.1), custom_call_target="tpu_custom_call" | custom-call | tf_op jit(solution)/shard_map/pallas_call | solution.py:668

commit v5 on v4

--- a/solution.py
+++ b/solution.py
@@ -225,18 +225,6 @@
         start = side * (w_ref.shape[0] // 2) + i * piece_rows
         return ref.at[pl.ds(pl.multiple_of(start, 16), piece_rows)]
 
-    @pl.when(dp == 0)
-    def _():
-        for i in range(pieces):
-            src, dst = piece_of(w_ref, 0, i), piece_of(wall.at[tp], 0, i)
-            send(src, dst, wa_s.at[i], wa_r.at[i], down)
-
-    @pl.when(dp == n_dp - 1)
-    def _():
-        for i in range(pieces):
-            src, dst = piece_of(w_ref, 1, i), piece_of(wall.at[tp], 1, i)
-            send(src, dst, wb_s.at[i], wb_r.at[i], up)
-
     def relay(slot):
         for side, hop, s_sem, r_sem, target in (
             (0, n_dp - 1 - dp, wa_s, wa_r, down),
@@ -272,6 +260,18 @@
     for o in near[3:]:
         kv_to_head(o)
 
+    @pl.when(dp == 0)
+    def _():
+        for i in range(pieces):
+            src, dst = piece_of(w_ref, 0, i), piece_of(wall.at[tp], 0, i)
+            send(src, dst, wa_s.at[i], wa_r.at[i], down)
+
+    @pl.when(dp == n_dp - 1)
+    def _():
+        for i in range(pieces):
+            src, dst = piece_of(w_ref, 1, i), piece_of(wall.at[tp], 1, i)
+            send(src, dst, wb_s.at[i], wb_r.at[i], up)
+
     def spread(s):
         wait_for(kvbuf.at[x, s], kv_r.at[x, s])
         send(kvbuf.at[x, s], kvbuf.at[x, s], xr_s.at[s], kv_r.at[x, s], right)
@@ -299,12 +299,10 @@
         ys = 2 * ((y // 2 + i + 1) % half) + core
         wait_for(qbuf.at[ys], q_r.at[ys])
         send(qbuf.at[ys], qbuf.at[ys], qf_s.at[i], q_r.at[ys], sibling)
-    relay(0)
     own_g.wait()
     relayout(0)
     spread(1)
     send(w_ref, wall.at[tp], w_s, w_r, sibling)
-    relay(1)
     relayout(1)
     pass_on(0)
     for i in range(half):
@@ -324,7 +322,6 @@
         )
 
     pass_on(1)
-    relay(2)
     relayout(2)
     factor = math.log2(math.e) / math.sqrt(HD)
     hr_rows = rows // 2
@@ -380,23 +377,23 @@
             acc[at] = mix
             top[at] = jnp.broadcast_to(new, (wide, LANES))
 
+    relay(0)
     arrive(x_left, 1)
     attend((x, x_left), 0, True)
-    relay(3)
+    relay(1)
     spread(2)
     relayout(3)
     spread(3)
-    relay(4)
     arrive(x_right, 0)
     arrive(x_far, 0)
     arrive(x_far, 1)
     attend((x_right, x_far), 0, False)
+    relay(2)
     pass_on(2)
     pass_on(3)
-    relay(5)
     arrive(x_left, 3)
     attend((x, x_left), 2, False)
-    relay(6)
+    relay(3)
     arrive(x_right, 2)
     arrive(x_far, 2)
     arrive(x_far, 3)
@@ -407,11 +404,12 @@
         at, mix, new = tile(last, 2, (1 - core) * half * rows + t * wide, False)
         acc[at] = jnp.where(lane >= LANES - 16, jnp.broadcast_to(new, (wide, LANES)), mix)
         send(acc.at[at], accr.at[pl.ds(t * wide, wide)], a_s.at[t], a_r.at[t], sibling)
-    relay(7)
+    relay(4)
     for t in range(half // 2):
         at, mix, new = tile(last, 2, core * half * rows + t * wide, False)
         acc[at] = mix
         top[at] = jnp.broadcast_to(new, (wide, LANES))
+    relay(5)
     for t in range(half // 2):
         wait_for(accr.at[pl.ds(t * wide, wide)], a_r.at[t])
         for k in range(2 * t, 2 * t + 2):
@@ -437,8 +435,7 @@
                     dev(yd, x, zh * 2 + cc),
                 )
 
-    for slot in range(n_dp + 4, n_dp + pieces - 1):
-        relay(slot)
+    relay(6)
     for load in (own_w, own_x, own_x2, load_gain, load_bias):
         load.wait()
     wait_for(wall.at[zh * 2 + 1 - core], w_r)
@@ -448,8 +445,11 @@
             wait_for(cbuf.at[g * half + j], c_r.at[g * half + j])
             cat[zh, g, :, HD * j : HD * (j + 1)] = cbuf[g * half + j, :, 0:HD]
         send(cat.at[zh, g], cat.at[zh, g], z_s.at[g], z_r.at[g], partner)
+    relay(7)
     for g in range(2):
         total += jnp.dot(cat[zh, g], wall[zh * 2 + g], preferred_element_type=F32)
+    for slot in range(8, n_dp + pieces - 1):
+        relay(slot)
     for side in range(2):
         for i in range(pieces):
             wait_for(piece_of(wall.at[away_sibling], side, i), wf_r.at[side, i])

time: 77.4 us -> 77.7 us (level)
  the two profiles are of different devices: /device:TPU:23 before, /device:TPU:8 now
where the time goes in v5:
time: 77.7 us; the launch traced here: 77.5 us
  Pallas kernels  76.9 us (99%)
    pallas_call x1, Pallas kernels, shards(): pl.pallas_call(functools.partial(kernel, ny, nx), out_shape=(jax.ShapeDty...  73.7 us
    pallas_call x1, Pallas kernels, shards(): pl.pallas_call(convolve, out_shape=(jax.ShapeDtypeStruct((block, model),...  3.21 us

profile of v5, /device:TPU:8, one launch (start us, length us, event | category | flops | bytes accessed | tf_op | source)
XLA Modules:
  0.0 77.5 jit_solution(3871242147968745042)
XLA Ops:
  0.6 73.7 %shard_map.122 = (bf16[48,1536]{1,0:T(8,128)(2,1)}, f32[224,384]{1,0:T(8,128)}) custom-call(bf16[192,1536]{1,0:T(8,128)(2,1)} %resid_in.1, bf16[192,384]{1,0:T(8,128)(2,1)} %q_in.1, bf16[192,384]{1,0:T(8,128)(2,1)} %k_in.1, bf16[192,384]{1,0:T(8,128)(2,1)} %v_in.1, bf16[384,1536]{1,0:T(8,128)(2,1)} %w_ref.1, f32[1536]{0:T(1024)} %gain_in.1, f32[1536]{0:T(1024)} %bias_in.1, ...), custom_call_target="tpu_custom_call" | custom-call | flops 3000000000 | bytes 10000000 | tf_op jit(solution)/shard_map/pallas_call | solution.py:643
  74.3 3.2 %shard_map.123 = (bf16[48,1536]{1,0:T(8,128)(2,1)}, bf16[192,384]{1,0:T(8,128)(2,1)}) custom-call(bf16[48,1536]{1,0:T(8,128)(2,1)} %get-tuple-element.4.att_in, f32[224,384]{1,0:T(8,128)} %get-tuple-element.5.gpad, f32[31,384]{1,0:T(8,128)} %taps_ref.1, f32[384]{0:T(512)} %scale_ref.1, f32[384]{0:T(512)} %shift_ref.1), custom_call_target="tpu_custom_call" | custom-call | tf_op jit(solution)/shard_map/pallas_call | solution.py:668

commit v6 on v5

--- a/solution.py
+++ b/solution.py
@@ -91,16 +91,15 @@
     c_s,
     c_r,
     w_s,
-    w_r,
+    ww_r,
     l_r,
     z_s,
     z_r,
     n_s,
     n_r,
     wa_s,
-    wa_r,
+    w_r,
     wb_s,
-    wb_r,
     wf_s,
     wf_r,
     h_s,
@@ -219,29 +218,35 @@
     for o in near[:3]:
         kv_to_head(o)
     pieces = wa_s.shape[0]
-    piece_rows = w_ref.shape[0] // (2 * pieces)
-
-    def piece_of(ref, side, i):
-        start = side * (w_ref.shape[0] // 2) + i * piece_rows
-        return ref.at[pl.ds(pl.multiple_of(start, 16), piece_rows)]
-
-    def relay(slot):
-        for side, hop, s_sem, r_sem, target in (
-            (0, n_dp - 1 - dp, wa_s, wa_r, down),
-            (1, dp, wb_s, wb_r, up),
-        ):
-            i = slot - hop
-
-            @pl.when(jnp.logical_and(i >= 0, i < pieces))
+    piece_rows = w_ref.shape[0] // pieces
+
+    def piece_of(ref, i):
+        return ref.at[i * piece_rows : (i + 1) * piece_rows]
+
+    low, high = dp == 0, dp == n_dp - 1
+    edge = jnp.logical_or(low, high)
+
+    def relay(i):
+        held = piece_of(wall.at[away], i)
+
+        @pl.when(edge)
+        def _():
+            wait_for(held, w_r.at[i])
+
+        for on, device in ((low, up), (high, down)):
+
+            @pl.when(on)
             def _():
-                held = piece_of(wall.at[away], side, i)
-                wait_for(held, r_sem.at[i])
-
-                @pl.when(hop < n_dp - 1)
-                def _():
-                    send(held, held, s_sem.at[i], r_sem.at[i], target)
-
-                send(held, held, wf_s.at[side, i], wf_r.at[side, i], sibling)
+                send(held, held, wb_s.at[i], w_r.at[i], device)
+
+    def share(i):
+        held = piece_of(wall.at[away], i)
+
+        @pl.when(jnp.logical_not(edge))
+        def _():
+            wait_for(held, w_r.at[i])
+
+        send(held, held, wf_s.at[i], wf_r.at[i], sibling)
 
     load_q.wait()
     for j in range(half):
@@ -260,17 +265,13 @@
     for o in near[3:]:
         kv_to_head(o)
 
-    @pl.when(dp == 0)
-    def _():
-        for i in range(pieces):
-            src, dst = piece_of(w_ref, 0, i), piece_of(wall.at[tp], 0, i)
-            send(src, dst, wa_s.at[i], wa_r.at[i], down)
-
-    @pl.when(dp == n_dp - 1)
-    def _():
-        for i in range(pieces):
-            src, dst = piece_of(w_ref, 1, i), piece_of(wall.at[tp], 1, i)
-            send(src, dst, wb_s.at[i], wb_r.at[i], up)
+    for on, device in ((low, down), (high, up)):
+
+        @pl.when(on)
+        def _():
+            for i in range(pieces):
+                src, dst = piece_of(w_ref, i), piece_of(wall.at[tp], i)
+                send(src, dst, wa_s.at[i], w_r.at[i], device)
 
     def spread(s):
         wait_for(kvbuf.at[x, s], kv_r.at[x, s])
@@ -302,7 +303,7 @@
     own_g.wait()
     relayout(0)
     spread(1)
-    send(w_ref, wall.at[tp], w_s, w_r, sibling)
+    send(w_ref, wall.at[tp], w_s, ww_r, sibling)
     relayout(1)
     pass_on(0)
     for i in range(half):
@@ -404,12 +405,13 @@
         at, mix, new = tile(last, 2, (1 - core) * half * rows + t * wide, False)
         acc[at] = jnp.where(lane >= LANES - 16, jnp.broadcast_to(new, (wide, LANES)), mix)
         send(acc.at[at], accr.at[pl.ds(t * wide, wide)], a_s.at[t], a_r.at[t], sibling)
-    relay(4)
     for t in range(half // 2):
         at, mix, new = tile(last, 2, core * half * rows + t * wide, False)
         acc[at] = mix
         top[at] = jnp.broadcast_to(new, (wide, LANES))
-    relay(5)
+    relay(4)
+    for i in range(2):
+        share(i)
     for t in range(half // 2):
         wait_for(accr.at[pl.ds(t * wide, wide)], a_r.at[t])
         for k in range(2 * t, 2 * t + 2):
@@ -435,24 +437,24 @@
                     dev(yd, x, zh * 2 + cc),
                 )
 
-    relay(6)
+    relay(5)
+    share(2)
+    share(3)
     for load in (own_w, own_x, own_x2, load_gain, load_bias):
         load.wait()
-    wait_for(wall.at[zh * 2 + 1 - core], w_r)
+    wait_for(wall.at[zh * 2 + 1 - core], ww_r)
     total = resid[...].astype(F32)
     for g in range(2):
         for j in range(half):
             wait_for(cbuf.at[g * half + j], c_r.at[g * half + j])
             cat[zh, g, :, HD * j : HD * (j + 1)] = cbuf[g * half + j, :, 0:HD]
         send(cat.at[zh, g], cat.at[zh, g], z_s.at[g], z_r.at[g], partner)
-    relay(7)
     for g in range(2):
         total += jnp.dot(cat[zh, g], wall[zh * 2 + g], preferred_element_type=F32)
-    for slot in range(8, n_dp + pieces - 1):
-        relay(slot)
-    for side in range(2):
-        for i in range(pieces):
-            wait_for(piece_of(wall.at[away_sibling], side, i), wf_r.at[side, i])
+    for i in range(4, pieces):
+        share(i)
+    for i in range(pieces):
+        wait_for(piece_of(wall.at[away_sibling], i), wf_r.at[i])
     for g in range(2):
         wait_for(cat.at[1 - zh, g], z_r.at[g])
         total += jnp.dot(cat[1 - zh, g], wall[(1 - zh) * 2 + g], preferred_element_type=F32)
@@ -521,10 +523,13 @@
     for t in range(half // 2):
         wait_for(accr.at[pl.ds(t * wide, wide)], a_s.at[t])
     for i in range(pieces):
-        wait_for(piece_of(w_ref, 0, i), wa_s.at[i])
-        wait_for(piece_of(w_ref, 1, i), wb_s.at[i])
-        for side in range(2):
-            wait_for(piece_of(w_ref, side, i), wf_s.at[side, i])
+        wait_for(piece_of(w_ref, i), wf_s.at[i])
+
+        @pl.when(edge)
+        def _():
+            wait_for(piece_of(w_ref, i), wa_s.at[i])
+            wait_for(piece_of(w_ref, i), wb_s.at[i])
+
     for g in range(2):
         wait_for(cat.at[zh, g], z_s.at[g])
     wait_for(nbuf.at[core], n_s)
@@ -635,8 +640,7 @@
         dma((pieces,)),
         dma((pieces,)),
         dma((pieces,)),
-        dma((2, pieces)),
-        dma((2, pieces)),
+        dma((pieces,)),
         dma((2,)),
         dma((2,)),
     ]

time: 77.7 us -> 73.1 us (0.941)
  Pallas kernels: 76.9 us -> 72.4 us
    pallas_call x1, Pallas kernels: 73.7 us -> 69.2 us  [shards(): pl.pallas_call(functools.partial(kernel, ny, nx), out_shape=(jax.ShapeDty...]
where the time goes in v6:
time: 73.1 us; the launch traced here: 73 us
  Pallas kernels  72.4 us (99%)
    pallas_call x1, Pallas kernels, shards(): pl.pallas_call(functools.partial(kernel, ny, nx), out_shape=(jax.ShapeDty...  69.2 us
    pallas_call x1, Pallas kernels, shards(): pl.pallas_call(convolve, out_shape=(jax.ShapeDtypeStruct((block, model),...  3.21 us

profile of v6, /device:TPU:8, one launch (start us, length us, event | category | flops | bytes accessed | tf_op | source)
XLA Modules:
  0.0 73.0 jit_solution(18327228074598042722)
XLA Ops:
  0.6 69.2 %shard_map.122 = (bf16[48,1536]{1,0:T(8,128)(2,1)}, f32[224,384]{1,0:T(8,128)}) custom-call(bf16[192,1536]{1,0:T(8,128)(2,1)} %resid_in.1, bf16[192,384]{1,0:T(8,128)(2,1)} %q_in.1, bf16[192,384]{1,0:T(8,128)(2,1)} %k_in.1, bf16[192,384]{1,0:T(8,128)(2,1)} %v_in.1, bf16[384,1536]{1,0:T(8,128)(2,1)} %w_ref.1, f32[1536]{0:T(1024)} %gain_in.1, f32[1536]{0:T(1024)} %bias_in.1, ...), custom_call_target="tpu_custom_call" | custom-call | flops 3000000000 | bytes 10000000 | tf_op jit(solution)/shard_map/pallas_call | solution.py:647
  69.8 3.2 %shard_map.123 = (bf16[48,1536]{1,0:T(8,128)(2,1)}, bf16[192,384]{1,0:T(8,128)(2,1)}) custom-call(bf16[48,1536]{1,0:T(8,128)(2,1)} %get-tuple-element.4.att_in, f32[224,384]{1,0:T(8,128)} %get-tuple-element.5.gpad, f32[31,384]{1,0:T(8,128)} %taps_ref.1, f32[384]{0:T(512)} %scale_ref.1, f32[384]{0:T(512)} %shift_ref.1), custom_call_target="tpu_custom_call" | custom-call | tf_op jit(solution)/shard_map/pallas_call | solution.py:672

commit v7 on v6

--- a/solution.py
+++ b/solution.py
@@ -131,7 +131,7 @@
     up = (above % n_dp, ctx, above // n_dp * 2 + core)
     down = (below % n_dp, ctx, below // n_dp * 2 + core)
     x_right, x_left, x_far = (x + 1) % nx, (x + nx - 1) % nx, (x + 2) % nx
-    right, left = dev(y, x_right, tp), dev(y, x_left, tp)
+    right, left, far = dev(y, x_right, tp), dev(y, x_left, tp), dev(y, x_far, tp)
 
     loads = [
         pltpu.make_async_copy(src, dst, l_r.at[i])
@@ -168,6 +168,7 @@
     greet(up)
     greet(down)
     greet(right)
+    greet(far)
     greet(left)
     greet((dp, (ctx + 1) % n_ctx, tp))
     greet((dp, (ctx + n_ctx - 1) % n_ctx, tp))
@@ -186,7 +187,7 @@
             axis=1,
         )
 
-    pl.semaphore_wait(barrier, 2 * (ny - 1) + 8)
+    pl.semaphore_wait(barrier, 2 * (ny - 1) + 9)
 
     def rank(distance):
         sign = distance // (half + 1)
@@ -277,11 +278,7 @@
         wait_for(kvbuf.at[x, s], kv_r.at[x, s])
         send(kvbuf.at[x, s], kvbuf.at[x, s], xr_s.at[s], kv_r.at[x, s], right)
         send(kvbuf.at[x, s], kvbuf.at[x, s], xl_s.at[s], kv_r.at[x, s], left)
-
-    def pass_on(s):
-        slot, target = (x_left, right) if s % 2 == 0 else (x_right, left)
-        wait_for(kvbuf.at[slot, s], kv_r.at[slot, s])
-        send(kvbuf.at[slot, s], kvbuf.at[slot, s], xf_s.at[s], kv_r.at[slot, s], target)
+        send(kvbuf.at[x, s], kvbuf.at[x, s], xf_s.at[s], kv_r.at[x, s], far)
 
     def arrive(slot, s):
         wait_for(kvbuf.at[slot, s], kv_r.at[slot, s])
@@ -302,10 +299,10 @@
         send(qbuf.at[ys], qbuf.at[ys], qf_s.at[i], q_r.at[ys], sibling)
     own_g.wait()
     relayout(0)
+    relay(0)
     spread(1)
     send(w_ref, wall.at[tp], w_s, ww_r, sibling)
     relayout(1)
-    pass_on(0)
     for i in range(half):
         ys = 2 * ((y // 2 + i) % half) + 1 - core
         wait_for(qbuf.at[ys], q_r.at[ys])
@@ -322,7 +319,6 @@
             axis=1,
         )
 
-    pass_on(1)
     relayout(2)
     factor = math.log2(math.e) / math.sqrt(HD)
     hr_rows = rows // 2
@@ -378,24 +374,26 @@
             acc[at] = mix
             top[at] = jnp.broadcast_to(new, (wide, LANES))
 
-    relay(0)
+    relay(1)
+    arrive(x_left, 0)
     arrive(x_left, 1)
     attend((x, x_left), 0, True)
-    relay(1)
+    relay(2)
     spread(2)
     relayout(3)
     spread(3)
     arrive(x_right, 0)
+    arrive(x_right, 1)
     arrive(x_far, 0)
     arrive(x_far, 1)
     attend((x_right, x_far), 0, False)
-    relay(2)
-    pass_on(2)
-    pass_on(3)
+    relay(3)
+    arrive(x_left, 2)
     arrive(x_left, 3)
     attend((x, x_left), 2, False)
-    relay(3)
+    relay(4)
     arrive(x_right, 2)
+    arrive(x_right, 3)
     arrive(x_far, 2)
     arrive(x_far, 3)
     last = (x_right, x_far)
@@ -409,7 +407,7 @@
         at, mix, new = tile(last, 2, core * half * rows + t * wide, False)
         acc[at] = mix
         top[at] = jnp.broadcast_to(new, (wide, LANES))
-    relay(4)
+    relay(5)
     for i in range(2):
         share(i)
     for t in range(half // 2):
@@ -437,7 +435,6 @@
                     dev(yd, x, zh * 2 + cc),
                 )
 
-    relay(5)
     share(2)
     share(3)
     for load in (own_w, own_x, own_x2, load_gain, load_bias):

time: 73.1 us -> 70 us (0.958)
  the two profiles are of different devices: /device:TPU:8 before, /device:TPU:15 now
where the time goes in v7:
time: 70 us; the launch traced here: 69.9 us
  Pallas kernels  69.3 us (99%)
    pallas_call x1, Pallas kernels, shards(): pl.pallas_call(functools.partial(kernel, ny, nx), out_shape=(jax.ShapeDty...  66.1 us
    pallas_call x1, Pallas kernels, shards(): pl.pallas_call(convolve, out_shape=(jax.ShapeDtypeStruct((block, model),...  3.21 us

profile of v7, /device:TPU:15, one launch (start us, length us, event | category | flops | bytes accessed | tf_op | source)
XLA Modules:
  0.0 69.9 jit_solution(1558528945912509935)
XLA Ops:
  0.6 66.1 %shard_map.122 = (bf16[48,1536]{1,0:T(8,128)(2,1)}, f32[224,384]{1,0:T(8,128)}) custom-call(bf16[192,1536]{1,0:T(8,128)(2,1)} %resid_in.1, bf16[192,384]{1,0:T(8,128)(2,1)} %q_in.1, bf16[192,384]{1,0:T(8,128)(2,1)} %k_in.1, bf16[192,384]{1,0:T(8,128)(2,1)} %v_in.1, bf16[384,1536]{1,0:T(8,128)(2,1)} %w_ref.1, f32[1536]{0:T(1024)} %gain_in.1, f32[1536]{0:T(1024)} %bias_in.1, ...), custom_call_target="tpu_custom_call" | custom-call | flops 3000000000 | bytes 10000000 | tf_op jit(solution)/shard_map/pallas_call | solution.py:644
  66.7 3.2 %shard_map.123 = (bf16[48,1536]{1,0:T(8,128)(2,1)}, bf16[192,384]{1,0:T(8,128)(2,1)}) custom-call(bf16[48,1536]{1,0:T(8,128)(2,1)} %get-tuple-element.4.att_in, f32[224,384]{1,0:T(8,128)} %get-tuple-element.5.gpad, f32[31,384]{1,0:T(8,128)} %taps_ref.1, f32[384]{0:T(512)} %scale_ref.1, f32[384]{0:T(512)} %shift_ref.1), custom_call_target="tpu_custom_call" | custom-call | tf_op jit(solution)/shard_map/pallas_call | solution.py:669
